TPU v7x, 128 devices: a whole 4x4x4 slice. The times are simulated.
128 devices in a mesh: expert: 32 (over z, y, core), shard: 4 (over x).
Axes of the slice: x: 4, y: 4, z: 4, core: 2. Of those that a mesh axis runs over, the one named last changes fastest.
Arguments:
- tokens: bfloat16 [32768, 1024], P(('expert', 'shard')), may hold values from -6 to 6
- lengths: int32 [32, 4], P('expert'), may hold values from 1 to 1020, as said below
- routes: int32 [32768, 8], P(('expert', 'shard')), may hold values from 0 to 31, all different within a row; in each aligned block of 256 rows (0 to 255, 256 to 511, ...) at most 96 rows name the same one
- norm1_gain: bfloat16 [1024], P('shard'), may hold values from 0.5 to 1.5
- w_query: bfloat16 [1024, 1024], P('shard'), may hold values from -0.1875 to 0.1875
- w_key: bfloat16 [1024, 512], P('shard'), may hold values from -0.1875 to 0.1875
- w_value: bfloat16 [1024, 512], P('shard'), may hold values from -0.1875 to 0.1875
- query_gain: bfloat16 [64], P('shard'), may hold values from 0.5 to 1.5
- key_gain: bfloat16 [64], P('shard'), may hold values from 0.5 to 1.5
- w_out: bfloat16 [1024, 1024], P('shard'), may hold values from -3 to 3
- norm2_gain: bfloat16 [1024], P('shard'), may hold values from 0.5 to 1.5
- w_router: bfloat16 [1024, 32], P('shard'), may hold values from -0.09375 to 0.09375
- w_gate: bfloat16 [32, 1024, 512], P('expert', None, 'shard'), may hold values from -0.1875 to 0.1875
- w_up: bfloat16 [32, 1024, 512], P('expert', None, 'shard'), may hold values from -0.1875 to 0.1875
- w_down: bfloat16 [32, 512, 1024], P('expert', 'shard'), may hold values from -0.75 to 0.75
- cotangent: bfloat16 [32768, 1024], P(('expert', 'shard')), may hold values from -6 to 6
Outputs:
- layer_out: bfloat16 [32768, 1024], P(('expert', 'shard'))
- tokens_grad: float32 [32768, 1024], P(('expert', 'shard'))
- norm1_gain_grad: float32 [1024], P('shard')
- w_query_grad: float32 [1024, 1024], P('shard')
- w_key_grad: float32 [1024, 512], P('shard')
- w_value_grad: float32 [1024, 512], P('shard')
- query_gain_grad: float32 [64], P('shard')
- key_gain_grad: float32 [64], P('shard')
- w_out_grad: float32 [1024, 1024], P('shard')
- norm2_gain_grad: float32 [1024], P('shard')
- w_router_grad: float32 [1024, 32], P('shard')
- w_gate_grad: float32 [32, 1024, 512], P('expert', None, 'shard')
- w_up_grad: float32 [32, 1024, 512], P('expert', None, 'shard')
- w_down_grad: float32 [32, 512, 1024], P('expert', 'shard')
Inputs may be any that keep to these rules, and one draw needn't show every extreme that they name: `lengths`: lengths of a sequence sum to less than 1024, so each ends in padding; one document of each sequence is longer than 768. `routes`: each row names 8 different experts; the rows of one device name no expert more than 96 times.
All inputs are finite; a program needn't handle non-finite values.
Results may differ from a plain program's by a relative error of at most 0.025.
Values may be sent and summed in bfloat16 or wider, within the bound.
A program may use at most 256 MiB of HBM per device.

v0:
```python
import math

import jax
import jax.numpy as jnp
from jax import lax
from jax.sharding import PartitionSpec as P

CAP = 96


EPS = 1e-06
ROPE_BASE = 10000.0


def rms_norm(values, gain):
    inv_rms = lax.rsqrt(jnp.mean(values * values, axis=-1, keepdims=True) + EPS)
    return values * inv_rms * gain


def rope_tables(positions, head_dim):
    half_dim = head_dim // 2
    frequency = ROPE_BASE ** (-(jnp.arange(half_dim, dtype=jnp.float32) * (2.0 / head_dim)))
    angles = positions.astype(jnp.float32)[:, None] * frequency[None, :]
    return (jnp.cos(angles), jnp.sin(angles))


def rotate(values, cosine, sine_table):
    half_dim = values.shape[-1] // 2
    lower_half = values[..., :half_dim]
    upper_half = values[..., half_dim:]
    cosine = cosine[:, None, :]
    sine_table = sine_table[:, None, :]
    return jnp.concatenate(
        [
            lower_half * cosine - upper_half * sine_table,
            upper_half * cosine + lower_half * sine_table,
        ],
        axis=-1,
    )


def layout(lengths_row, positions):
    doc_ends = jnp.cumsum(lengths_row)
    passed = positions[:, None] >= doc_ends[None, :]
    doc_ids = jnp.sum(passed.astype(jnp.int32), axis=1)
    doc_start = jnp.sum(jnp.where(passed, lengths_row[None, :], 0), axis=1)
    return (doc_ids, positions - doc_start)


def softmax_last(chosen):
    return jax.nn.softmax(chosen, axis=-1)


def swiglu(gate_pre, up_pre):
    return jax.nn.silu(gate_pre) * up_pre


def pack_rows(route_rows, flat_experts, slots, experts, capacity):
    buffer = jnp.zeros((experts, capacity, route_rows.shape[1]), route_rows.dtype)
    return buffer.at[flat_experts, slots].set(route_rows)


def masked_scores(query_low, keys_low, same_doc, kv_heads, head_dim):
    grouped = query_low.reshape(query_low.shape[0], kv_heads, -1, head_dim)
    keyed = keys_low.reshape(keys_low.shape[0], kv_heads, head_dim)
    scores = jnp.einsum(
        "tkgd,skd->kgts", grouped, keyed, preferred_element_type=jnp.float32
    ) / math.sqrt(head_dim)
    return jnp.where(same_doc[None, None], scores, -1e30)


def expert_front(expert_inputs, gate_full, up_full):
    gate_pre = jnp.einsum(
        "erd,edf->erf", expert_inputs, gate_full, preferred_element_type=jnp.float32
    )
    up_pre = jnp.einsum("erd,edf->erf", expert_inputs, up_full, preferred_element_type=jnp.float32)
    return jax.vjp(swiglu, gate_pre, up_pre)


def body(
    tokens,
    lengths,
    routes,
    norm1_gain,
    w_query,
    w_key,
    w_value,
    query_gain,
    key_gain,
    w_out,
    norm2_gain,
    w_router,
    w_gate,
    w_up,
    w_down,
    cotangent,
):
    highest = lax.Precision.HIGHEST
    row_count = tokens.shape[0]
    width = tokens.shape[1]
    shards = lax.axis_size("shard")
    length = row_count * shards
    (
        query_full,
        key_full,
        value_full,
        out_full,
        router_full,
        gain_first,
        gain_second,
        gain_query,
        gain_key,
    ) = (
        lax.all_gather(w_query, "shard", axis=0, tiled=True),
        lax.all_gather(w_key, "shard", axis=0, tiled=True),
        lax.all_gather(w_value, "shard", axis=0, tiled=True),
        lax.all_gather(w_out, "shard", axis=0, tiled=True),
        lax.all_gather(w_router, "shard", axis=0, tiled=True),
        lax.all_gather(norm1_gain, "shard", axis=0, tiled=True),
        lax.all_gather(norm2_gain, "shard", axis=0, tiled=True),
        lax.all_gather(query_gain, "shard", axis=0, tiled=True),
        lax.all_gather(key_gain, "shard", axis=0, tiled=True),
    )
    gain_first = gain_first.astype(jnp.float32)
    gain_second = gain_second.astype(jnp.float32)
    gain_query = gain_query.astype(jnp.float32)
    gain_key = gain_key.astype(jnp.float32)
    head_dim = gain_query.shape[0]
    heads = query_full.shape[1] // head_dim
    kv_heads = key_full.shape[1] // head_dim
    group = heads // kv_heads
    experts = router_full.shape[1]
    topk = routes.shape[1]
    docs = lengths.shape[1]
    inv_root = 1.0 / math.sqrt(head_dim)
    tokens_float = tokens.astype(jnp.float32)
    normed_one, norm_one_back = jax.vjp(rms_norm, tokens_float, gain_first)
    normed_low = normed_one.astype(jnp.bfloat16)
    query_pre = jnp.dot(normed_low, query_full, preferred_element_type=jnp.float32)
    key_pre = jnp.dot(normed_low, key_full, preferred_element_type=jnp.float32)
    value_pre = jnp.dot(normed_low, value_full, preferred_element_type=jnp.float32)
    positions = lax.axis_index("shard") * row_count + jnp.arange(row_count, dtype=jnp.int32)
    doc_query, rope_pos = layout(lengths[0], positions)
    doc_key = layout(lengths[0], jnp.arange(length, dtype=jnp.int32))[0]
    cosine, sine_table = rope_tables(rope_pos, head_dim)

    def shape_heads(query_in, key_in, gain_q, gain_k):
        query_rot = rotate(
            rms_norm(query_in.reshape(row_count, heads, head_dim), gain_q), cosine, sine_table
        )
        key_rot = rotate(
            rms_norm(key_in.reshape(row_count, kv_heads, head_dim), gain_k), cosine, sine_table
        )
        return (
            query_rot.reshape(row_count, heads * head_dim),
            key_rot.reshape(row_count, kv_heads * head_dim),
        )

    (query_rot, key_rot), heads_back = jax.vjp(
        shape_heads, query_pre, key_pre, gain_query, gain_key
    )
    query_low = query_rot.astype(jnp.bfloat16)
    key_low = key_rot.astype(jnp.bfloat16)
    value_low = value_pre.astype(jnp.bfloat16)
    keys_all, values_all = (
        lax.all_gather(key_low, "shard", axis=0, tiled=True),
        lax.all_gather(value_low, "shard", axis=0, tiled=True),
    )
    same_doc = doc_query[:, None] == doc_key[None, :]
    live_rows = (doc_query < docs)[:, None]
    scores = masked_scores(query_low, keys_all, same_doc, kv_heads, head_dim)
    top_score = jnp.max(scores, axis=-1, keepdims=True)
    exponent_terms = jnp.exp(scores - top_score)
    denominator = jnp.sum(exponent_terms, axis=-1, keepdims=True)
    probs_low = (exponent_terms / denominator).astype(jnp.bfloat16)
    log_total = top_score + jnp.log(denominator)
    attn_mixed = jnp.einsum(
        "kgts,skd->tkgd",
        probs_low,
        values_all.reshape(length, kv_heads, head_dim),
        preferred_element_type=jnp.float32,
    ).reshape(row_count, heads * head_dim)
    mixed_low = jnp.where(live_rows, attn_mixed, 0.0).astype(jnp.bfloat16)
    middle = tokens_float + jnp.dot(mixed_low, out_full, preferred_element_type=jnp.float32)
    normed_two, norm_two_back = jax.vjp(rms_norm, middle, gain_second)
    routed_low = normed_two.astype(jnp.bfloat16)
    logits = jnp.dot(routed_low, router_full, preferred_element_type=jnp.float32)
    selector = (routes[:, :, None] == jnp.arange(experts, dtype=jnp.int32)[None, None, :]).astype(
        jnp.float32
    )
    chosen = jnp.einsum("te,tke->tk", logits, selector, precision=highest)
    gate_weights, router_back = jax.vjp(softmax_last, chosen)
    flat_experts = routes.reshape(-1)
    route_hits = (flat_experts[:, None] == jnp.arange(experts, dtype=jnp.int32)[None, :]).astype(
        jnp.int32
    )
    slots = jnp.sum((jnp.cumsum(route_hits, axis=0) - route_hits) * route_hits, axis=1)
    route_rows = jnp.broadcast_to(routed_low[:, None, :], (row_count, topk, width)).reshape(
        row_count * topk, width
    )
    received = lax.all_to_all(
        pack_rows(route_rows, flat_experts, slots, experts, CAP),
        "expert",
        split_axis=0,
        concat_axis=1,
        tiled=True,
    )
    gate_full, up_full, down_full = (
        lax.all_gather(w_gate, "shard", axis=2, tiled=True),
        lax.all_gather(w_up, "shard", axis=2, tiled=True),
        lax.all_gather(w_down, "shard", axis=1, tiled=True),
    )
    activated, swiglu_back = expert_front(received, gate_full, up_full)
    act_low = activated.astype(jnp.bfloat16)
    expert_rows = jnp.einsum(
        "erf,efd->erd", act_low, down_full, preferred_element_type=jnp.float32
    ).astype(jnp.bfloat16)
    returned = lax.all_to_all(expert_rows, "expert", split_axis=1, concat_axis=0, tiled=True)
    route_float = returned[flat_experts, slots].reshape(row_count, topk, width).astype(jnp.float32)
    expert_mix = jnp.sum(gate_weights[:, :, None] * route_float, axis=1)
    result = (middle + expert_mix).astype(jnp.bfloat16)
    grad_result = cotangent.astype(jnp.float32)
    grad_gates = jnp.sum(grad_result[:, None, :] * route_float, axis=-1)
    grad_routes = (
        (gate_weights[:, :, None] * grad_result[:, None, :])
        .astype(jnp.bfloat16)
        .reshape(row_count * topk, width)
    )
    grad_received = lax.all_to_all(
        pack_rows(grad_routes, flat_experts, slots, experts, CAP),
        "expert",
        split_axis=0,
        concat_axis=1,
        tiled=True,
    )
    grad_act = jnp.einsum(
        "erd,efd->erf", grad_received, down_full, preferred_element_type=jnp.float32
    )
    grad_gate_pre, grad_up_pre = swiglu_back(grad_act)
    grad_gate_low = grad_gate_pre.astype(jnp.bfloat16)
    grad_up_low = grad_up_pre.astype(jnp.bfloat16)
    grad_down_w = jnp.einsum(
        "erf,erd->efd", act_low, grad_received, preferred_element_type=jnp.float32
    )
    grad_gate_w = jnp.einsum(
        "erd,erf->edf", received, grad_gate_low, preferred_element_type=jnp.float32
    )
    grad_up_w = jnp.einsum(
        "erd,erf->edf", received, grad_up_low, preferred_element_type=jnp.float32
    )
    grad_inputs = (
        jnp.einsum("erf,edf->erd", grad_gate_low, gate_full, preferred_element_type=jnp.float32)
        + jnp.einsum("erf,edf->erd", grad_up_low, up_full, preferred_element_type=jnp.float32)
    ).astype(jnp.bfloat16)
    gate_grad_out, up_grad_out, down_grad_out = (
        lax.psum_scatter(
            grad_gate_w.astype(jnp.bfloat16), "shard", scatter_dimension=2, tiled=True
        ).astype(jnp.float32),
        lax.psum_scatter(
            grad_up_w.astype(jnp.bfloat16), "shard", scatter_dimension=2, tiled=True
        ).astype(jnp.float32),
        lax.psum_scatter(
            grad_down_w.astype(jnp.bfloat16), "shard", scatter_dimension=1, tiled=True
        ).astype(jnp.float32),
    )
    grad_back = lax.all_to_all(grad_inputs, "expert", split_axis=1, concat_axis=0, tiled=True)
    grad_routed = jnp.sum(
        grad_back[flat_experts, slots].reshape(row_count, topk, width).astype(jnp.float32), axis=1
    )
    grad_chosen = router_back(grad_gates)[0]
    grad_logits = jnp.einsum("tk,tke->te", grad_chosen, selector, precision=highest)
    grad_router = jnp.dot(
        routed_low.astype(jnp.float32).T,
        grad_logits,
        precision=highest,
        preferred_element_type=jnp.float32,
    )
    grad_routed = grad_routed + jnp.dot(
        grad_logits,
        router_full.astype(jnp.float32).T,
        precision=highest,
        preferred_element_type=jnp.float32,
    )
    grad_middle_norm, grad_gain_second = norm_two_back(grad_routed)
    grad_middle = grad_result + grad_middle_norm
    grad_attn_low = grad_middle.astype(jnp.bfloat16)
    grad_out_w = jnp.dot(mixed_low.T, grad_attn_low, preferred_element_type=jnp.float32)
    grad_mixed = jnp.dot(grad_attn_low, out_full.T, preferred_element_type=jnp.float32)
    grad_mixed_low = jnp.where(
        live_rows, grad_mixed.astype(jnp.bfloat16), jnp.zeros((), jnp.bfloat16)
    )
    scores_again = masked_scores(query_low, keys_all, same_doc, kv_heads, head_dim)
    attn_probs = jnp.exp(scores_again - log_total)
    grad_heads = grad_mixed_low.reshape(row_count, kv_heads, group, head_dim)
    keys_grouped = keys_all.reshape(length, kv_heads, head_dim)
    values_grouped = values_all.reshape(length, kv_heads, head_dim)
    query_grouped = query_low.reshape(row_count, kv_heads, group, head_dim)
    grad_probs = jnp.einsum(
        "tkgd,skd->kgts", grad_heads, values_grouped, preferred_element_type=jnp.float32
    )
    row_dot = jnp.sum(attn_probs * grad_probs, axis=-1, keepdims=True)
    grad_scores = jnp.where(same_doc[None, None], attn_probs * (grad_probs - row_dot), 0.0).astype(
        jnp.bfloat16
    )
    grad_values = jnp.einsum(
        "kgts,tkgd->skd",
        attn_probs.astype(jnp.bfloat16),
        grad_heads,
        preferred_element_type=jnp.float32,
    )
    grad_keys = (
        jnp.einsum("kgts,tkgd->skd", grad_scores, query_grouped, preferred_element_type=jnp.float32)
        * inv_root
    )
    grad_query = (
        jnp.einsum("kgts,skd->tkgd", grad_scores, keys_grouped, preferred_element_type=jnp.float32)
        * inv_root
    )
    own_keys, own_values = (
        lax.psum_scatter(
            grad_keys.reshape(length, kv_heads * head_dim).astype(jnp.bfloat16),
            "shard",
            scatter_dimension=0,
            tiled=True,
        ).astype(jnp.float32),
        lax.psum_scatter(
            grad_values.reshape(length, kv_heads * head_dim).astype(jnp.bfloat16),
            "shard",
            scatter_dimension=0,
            tiled=True,
        ).astype(jnp.float32),
    )
    grad_query_pre, grad_key_pre, grad_gain_query, grad_gain_key = heads_back(
        (grad_query.reshape(row_count, heads * head_dim), own_keys)
    )
    query_grad_low = grad_query_pre.astype(jnp.bfloat16)
    key_grad_low = grad_key_pre.astype(jnp.bfloat16)
    value_grad_low = own_values.astype(jnp.bfloat16)
    grad_query_w = jnp.dot(normed_low.T, query_grad_low, preferred_element_type=jnp.float32)
    grad_key_w = jnp.dot(normed_low.T, key_grad_low, preferred_element_type=jnp.float32)
    grad_value_w = jnp.dot(normed_low.T, value_grad_low, preferred_element_type=jnp.float32)
    grad_normed = (
        jnp.dot(query_grad_low, query_full.T, preferred_element_type=jnp.float32)
        + jnp.dot(key_grad_low, key_full.T, preferred_element_type=jnp.float32)
        + jnp.dot(value_grad_low, value_full.T, preferred_element_type=jnp.float32)
    )
    grad_tokens_norm, grad_gain_first = norm_one_back(grad_normed)
    grad_tokens = grad_middle + grad_tokens_norm
    (
        part_query,
        part_key,
        part_value,
        part_out,
        part_router,
        part_first,
        part_second,
        part_gq,
        part_gk,
    ) = (
        lax.psum_scatter(
            grad_query_w.astype(jnp.bfloat16), "shard", scatter_dimension=0, tiled=True
        ).astype(jnp.float32),
        lax.psum_scatter(
            grad_key_w.astype(jnp.bfloat16), "shard", scatter_dimension=0, tiled=True
        ).astype(jnp.float32),
        lax.psum_scatter(
            grad_value_w.astype(jnp.bfloat16), "shard", scatter_dimension=0, tiled=True
        ).astype(jnp.float32),
        lax.psum_scatter(
            grad_out_w.astype(jnp.bfloat16), "shard", scatter_dimension=0, tiled=True
        ).astype(jnp.float32),
        lax.psum_scatter(
            grad_router.astype(jnp.bfloat16), "shard", scatter_dimension=0, tiled=True
        ).astype(jnp.float32),
        lax.psum_scatter(
            grad_gain_first.astype(jnp.bfloat16), "shard", scatter_dimension=0, tiled=True
        ).astype(jnp.float32),
        lax.psum_scatter(
            grad_gain_second.astype(jnp.bfloat16), "shard", scatter_dimension=0, tiled=True
        ).astype(jnp.float32),
        lax.psum_scatter(
            grad_gain_query.astype(jnp.bfloat16), "shard", scatter_dimension=0, tiled=True
        ).astype(jnp.float32),
        lax.psum_scatter(
            grad_gain_key.astype(jnp.bfloat16), "shard", scatter_dimension=0, tiled=True
        ).astype(jnp.float32),
    )
    sum_query, sum_key, sum_value, sum_out, sum_router, sum_first, sum_second, sum_gq, sum_gk = (
        lax.psum(part_query.astype(jnp.bfloat16), "expert").astype(jnp.float32),
        lax.psum(part_key.astype(jnp.bfloat16), "expert").astype(jnp.float32),
        lax.psum(part_value.astype(jnp.bfloat16), "expert").astype(jnp.float32),
        lax.psum(part_out.astype(jnp.bfloat16), "expert").astype(jnp.float32),
        lax.psum(part_router.astype(jnp.bfloat16), "expert").astype(jnp.float32),
        lax.psum(part_first.astype(jnp.bfloat16), "expert").astype(jnp.float32),
        lax.psum(part_second.astype(jnp.bfloat16), "expert").astype(jnp.float32),
        lax.psum(part_gq.astype(jnp.bfloat16), "expert").astype(jnp.float32),
        lax.psum(part_gk.astype(jnp.bfloat16), "expert").astype(jnp.float32),
    )
    return (
        result,
        grad_tokens,
        sum_first,
        sum_query,
        sum_key,
        sum_value,
        sum_gq,
        sum_gk,
        sum_out,
        sum_second,
        sum_router,
        gate_grad_out,
        up_grad_out,
        down_grad_out,
    )


def solution(mesh):
    placed = (
        P(("expert", "shard"), None),
        P("expert", None),
        P(("expert", "shard"), None),
        P("shard"),
        P("shard", None),
        P("shard", None),
        P("shard", None),
        P("shard"),
        P("shard"),
        P("shard", None),
        P("shard"),
        P("shard", None),
        P("expert", None, "shard"),
        P("expert", None, "shard"),
        P("expert", "shard", None),
        P(("expert", "shard"), None),
    )
    return jax.shard_map(
        body,
        mesh=mesh,
        in_specs=placed,
        out_specs=(
            P(("expert", "shard"), None),
            P(("expert", "shard"), None),
            P("shard"),
            P("shard", None),
            P("shard", None),
            P("shard", None),
            P("shard"),
            P("shard"),
            P("shard", None),
            P("shard"),
            P("shard", None),
            P("expert", None, "shard"),
            P("expert", None, "shard"),
            P("expert", "shard", None),
        ),
        check_vma=False,
    )
```

profile of v0, /device:TPU:0, one launch (start us, length us, event | category | flops | bytes accessed | tf_op | source)
XLA Modules:
  0.0 1200.1 jit_solution(16619805443934609454)
XLA Ops:
  13.2 10.5 all-reduce.13
  39.9 22.2 %all-gather.12.cloned.1.call-done = bf16[1024,512]{1,0:T(8,128)(2,1)} async-done(((bf16[256,512]{1,0:T(8,128)(2,1)}), bf16[1024,512]{1,0:T(8,128)(2,1)}) %all-gather.12.cloned.1.call-update) | async-done | bytes 1048592 | tf_op jit(solution)/shard_map/all_gather | solution.py:116
  65.8 8.9 all-gather.1
  74.7 9.1 reduce-window.19
  85.7 9.2 all-gather.20.cloned.1.call-done
  99.0 23.9 %all-gather.18.cloned.1.call-done = bf16[1024,512]{0,1:T(8,128)(2,1)} async-done(((bf16[256,512]{0,1:T(8,128)(2,1)}), bf16[1024,512]{0,1:T(8,128)(2,1)}) %all-gather.18.cloned.1.call-update) | async-done | bytes 1048592 | tf_op jit(solution)/shard_map/all_gather | solution.py:166
  122.9 8.5 fusion.87
  131.5 18.5 %all-gather.14.cloned.1.call-done = bf16[1024,512]{1,0:T(8,128)(2,1)} async-done(((bf16[256,512]{1,0:T(8,128)(2,1)}), bf16[1024,512]{1,0:T(8,128)(2,1)}) %all-gather.14.cloned.1.call-update) | async-done | bytes 1048592 | tf_op jit(solution)/shard_map/all_gather | solution.py:167
  151.5 8.4 fusion.4
  159.9 7.8 fusion.13
  168.0 14.7 %all-gather.22.cloned.1.call-done = bf16[1024,1024]{1,0:T(8,128)(2,1)} async-done(((bf16[256,1024]{1,0:T(8,128)(2,1)}), bf16[1024,1024]{1,0:T(8,128)(2,1)}) %all-gather.22.cloned.1.call-update) | async-done | bytes 2097168 | tf_op jit(solution)/shard_map/all_gather | solution.py:117
  186.3 13.7 %scatter_custom_fusion = bf16[3072,1024]{1,0:T(8,128)(2,1)} fusion(s32[2048]{0:T(1024)S(1)} %broadcast_select_fusion, bf16[]{:T(256)} %constant.31.clone.1, bf16[256,1024]{1,0:T(8,128)(2,1)S(1)} %multiply_convert_fusion.2), kind=kCustom, calls=%fused_computation.41 | custom fusion | bytes 6815746
  207.7 11.9 all_gather.52
  221.8 14.7 %scatter_custom_fusion.1 = bf16[3072,1024]{1,0:T(8,128)(2,1)} fusion(s32[2048]{0:T(1024)S(1)} %broadcast_select_fusion, f32[256,1024]{1,0:T(8,128)S(1)} %convert_element_type.279, f32[2048]{0:T(1024)S(1)} %mul.518, bf16[]{:T(256)} %constant.31.clone.1), kind=kCustom, calls=%fused_computation.40 | custom fusion | flops 4194304 | bytes 7348226
  236.6 48.9 %all-to-all-done = bf16[32,96,1024]{2,1,0:T(8,128)(2,1)} async-done(((bf16[32,96,1024]{2,1,0:T(8,128)(2,1)}), bf16[32,96,1024]{2,1,0:T(8,128)(2,1)}, u32[]{:S(2)}, u32[]{:S(2)}) %all-to-all-start) | async-done | bytes 6291488 | tf_op jit(solution)/shard_map/all_to_all | solution.py:201
  292.6 26.2 %all-gather.26.cloned.1.call-done = bf16[1,1024,512]{2,1,0:T(8,128)(2,1)} async-done(((bf16[1,1024,128]{2,1,0:T(8,128)(2,1)}), bf16[1,1024,512]{2,1,0:T(8,128)(2,1)}) %all-gather.26.cloned.1.call-update) | async-done | bytes 1048592 | tf_op jit(solution)/shard_map/all_gather | solution.py:210
  318.8 9.1 fusion.51
  327.8 19.5 %all-gather.24.cloned.1.call-done = bf16[1,1024,512]{2,1,0:T(8,128)(2,1)} async-done(((bf16[1,1024,128]{2,1,0:T(8,128)(2,1)}), bf16[1,1024,512]{2,1,0:T(8,128)(2,1)}) %all-gather.24.cloned.1.call-update) | async-done | bytes 1048592 | tf_op jit(solution)/shard_map/all_gather | solution.py:209
  347.3 9.1 fusion.55
  356.4 17.6 %all-gather.28.cloned.1.call-done = bf16[1,512,1024]{2,1,0:T(8,128)(2,1)} async-done(((bf16[1,128,1024]{2,1,0:T(8,128)(2,1)}), bf16[1,512,1024]{2,1,0:T(8,128)(2,1)}) %all-gather.28.cloned.1.call-update) | async-done | bytes 1048592 | tf_op jit(solution)/shard_map/all_gather | solution.py:211
  374.0 14.9 %multiply_convert_fusion = (bf16[3072,512]{1,0:T(8,128)(2,1)}, bf16[3072,512]{1,0:T(8,128)(2,1)}, bf16[3072,512]{1,0:T(8,128)(2,1)S(1)}) fusion(f32[3072,512]{1,0:T(8,128)} %fusion.55, f32[3072,512]{1,0:T(8,128)} %fusion.51, bf16[3072,1024]{1,0:T(8,128)(2,1)} %bitcast.37, bf16[1,512,1024]{2,1,0:T(8,128)(2,1)} %all-gather.28.cloned.1.call-done), kind=kOutput, calls=%fused_computation.33 | convolution fusion | flops 3246391296 | bytes 29360128 | tf_op jit(solution)/shard_map/erd,efd->erf/dot_general | solution.py:236
  392.5 42.6 %copy.143 = bf16[1,3072,1024]{2,0,1:T(2,128)(2,1)} copy(bf16[1,3072,1024]{2,1,0:T(8,128)(2,1)S(1)} %convert_bitcast_fusion) | data formatting | bytes 12582912 | tf_op jit(solution)/shard_map/convert_element_type | solution.py:217
  435.6 37.7 %reduce.11 = bf16[3072,1024]{1,0:T(8,128)(2,1)} reduce(bf16[3072,1,1024]{2,1,0:T(2,128)(2,1)} %bitcast.236, bf16[]{:T(256)} %broadcast.378), dimensions={1}, to_apply=%bitcast.223.reduce_sub_computation | reduce | bytes 12582914
  473.4 13.0 %reshape.554 = bf16[32,2,49152]{2,1,0:T(2,128)(2,1)} reshape(bf16[3072,1024]{1,0:T(8,128)(2,1)} %reduce.11) | data formatting | bytes 12582912
  486.3 7.7 all-to-all-start.1
  494.1 8.4 fusion.53
  509.0 42.6 %copy.142 = bf16[1,3072,1024]{2,0,1:T(2,128)(2,1)} copy(bf16[1,3072,1024]{2,1,0:T(8,128)(2,1)S(1)} %fusion.17) | data formatting | bytes 12582912 | tf_op jit(solution)/shard_map/convert_element_type | solution.py:254
  551.6 37.8 %reduce.10 = bf16[3072,1024]{1,0:T(8,128)(2,1)} reduce(bf16[3072,1,1024]{2,1,0:T(2,128)(2,1)} %bitcast.237, bf16[]{:T(256)} %broadcast.378), dimensions={1}, to_apply=%bitcast.222.reduce_sub_computation | reduce | bytes 12582914
  589.4 13.0 %reshape.556 = bf16[32,2,49152]{2,1,0:T(2,128)(2,1)} reshape(bf16[3072,1024]{1,0:T(8,128)(2,1)} %reduce.10) | data formatting | bytes 12582912
  610.1 22.1 %reshape.555 = bf16[3072,1,1024]{2,1,0:T(2,128)(2,1)} reshape(bf16[32,2,49152]{2,1,0:T(2,128)(2,1)} %all-to-all-done.1) | data formatting | bytes 12582912
  632.1 9.8 copy.130
  641.9 40.7 %gather_fusion = bf16[2048,1024]{1,0:T(8,128)(2,1)} fusion(bf16[32,96,1024]{2,1,0:T(8,128)(2,1)} %bitcast.232, s32[2048]{0:T(1024)S(1)} %bitcast.230), kind=kCustom, calls=%fused_computation | custom fusion | bytes 8404992 | tf_op jit(solution)/shard_map/gather | solution.py:219
  690.2 21.7 %reshape.557 = bf16[3072,1,1024]{2,1,0:T(2,128)(2,1)} reshape(bf16[32,2,49152]{2,1,0:T(2,128)(2,1)} %all-to-all-done.3) | data formatting | bytes 12582912
  711.9 9.8 copy.131
  721.7 40.8 %gather_fusion.1 = bf16[2048,1024]{1,0:T(8,128)(2,1)} fusion(bf16[32,96,1024]{2,1,0:T(8,128)(2,1)} %bitcast.233, s32[2048]{0:T(1024)S(1)} %bitcast.231), kind=kCustom, calls=%fused_computation.1 | custom fusion | bytes 8404992 | tf_op jit(solution)/shard_map/gather | solution.py:268
  771.9 9.5 bitcast_convert_fusion
  781.5 8.1 fusion.89
  789.6 24.3 %fusion.29 = bf16[8,64,1024]{2,1,0:T(8,128)(2,1)} fusion(bf16[256,8,2,64]{0,3,2,1:T(8,128)(2,1)S(1)} %bitcast.254, f32[8,1024,256,2]{2,1,3,0:T(8,128)} %fusion.89, f32[8,2,256,1024]{2,3,1,0:T(8,128)} %get-tuple-element.66, f32[8,2,256]{2,1,0:T(2,128)S(1)} %bitcast.289, pred[256,1024]{0,1:T(8,128)(4,1)S(1)} %copy-done.19), kind=kOutput, calls=%fused_computation.49 | convolution fusion | flops 567284736 | bytes 35405824 | tf_op jit(solution)/shard_map/kgts,tkgd->skd/dot_general | solution.py:312
  842.8 8.3 fusion.35
  861.0 24.3 %fusion.36 = f32[8,64,2,256]{3,1,2,0:T(8,128)} fusion(bf16[1024,8,64,1]{0,2,3,1:T(8,128)(2,1)} %bitcast.261, f32[8,1024,256,2]{2,1,3,0:T(8,128)} %fusion.89, f32[8,2,256,1024]{2,3,1,0:T(8,128)} %get-tuple-element.66, f32[8,2,256]{2,1,0:T(2,128)S(1)} %bitcast.290, pred[256,1024]{0,1:T(8,128)(4,1)S(1)} %copy-done.19), kind=kOutput, calls=%fused_computation.72 | convolution fusion | flops 566498304 | bytes 35930112 | tf_op jit(solution)/shard_map/kgts,skd->tkgd/dot_general | solution.py:316
  901.3 13.5 %reduce-scatter.29.cloned.1.call-done = bf16[1,128,1024]{2,1,0:T(8,128)(2,1)} async-done(((bf16[1,512,1024]{2,1,0:T(8,128)(2,1)}), bf16[1,128,1024]{2,1,0:T(8,128)(2,1)}) %reduce-scatter.29.cloned.1.call-update) | async-done | bytes 262160 | tf_op jit(solution)/shard_map/reduce_scatter | solution.py:262
  921.9 19.2 %reduce-scatter.23.cloned.1.call-done = bf16[256,512]{1,0:T(8,128)(2,1)} async-done(((bf16[1024,512]{1,0:T(8,128)(2,1)}), bf16[256,512]{1,0:T(8,128)(2,1)}) %reduce-scatter.23.cloned.1.call-update) | async-done | bytes 262160 | tf_op jit(solution)/shard_map/reduce_scatter | solution.py:366
  941.0 26.1 %reduce-scatter.21.cloned.1.call-done = bf16[256,512]{1,0:T(8,128)(2,1)} async-done(((bf16[1024,512]{1,0:T(8,128)(2,1)}), bf16[256,512]{1,0:T(8,128)(2,1)}) %reduce-scatter.21.cloned.1.call-update) | async-done | bytes 262160 | tf_op jit(solution)/shard_map/reduce_scatter | solution.py:363
  967.2 31.8 %reduce-scatter.25.cloned.1.call-done = bf16[256,1024]{1,0:T(8,128)(2,1)} async-done(((bf16[1024,1024]{1,0:T(8,128)(2,1)}), bf16[256,1024]{1,0:T(8,128)(2,1)}) %reduce-scatter.25.cloned.1.call-update) | async-done | bytes 524304 | tf_op jit(solution)/shard_map/reduce_scatter | solution.py:369
  999.0 31.7 %reduce-scatter.19.cloned.1.call-done = bf16[256,1024]{1,0:T(8,128)(2,1)} async-done(((bf16[1024,1024]{1,0:T(8,128)(2,1)}), bf16[256,1024]{1,0:T(8,128)(2,1)}) %reduce-scatter.19.cloned.1.call-update) | async-done | bytes 524304 | tf_op jit(solution)/shard_map/reduce_scatter | solution.py:360
  1033.5 8.7 all-reduce.12
  1042.5 11.2 reduce-scatter.27.cloned.1.call-done
  1053.7 126.2 %all-reduce.10 = (bf16[256]{0:T(256)(128)(2,1)S(1)}, bf16[16]{0:T(256)(128)(2,1)S(1)}, bf16[16]{0:T(256)(128)(2,1)S(1)}, bf16[256]{0:T(256)(128)(2,1)S(1)}, bf16[256,32]{0,1:T(8,128)(2,1)S(1)}) all-reduce(bf16[256]{0:T(256)(128)(2,1)S(1)} %dynamic-slice.3, ...), channel_id=1, replica_groups=mesh['expert'=32,'shard'=4] {'expert'}, use_global_device_ids=true, to_apply=%region_30.31 | all-reduce | flops 8736 | bytes 34944 | tf_op jit(solution)/shard_map/psum | solution.py:394
  (329 shorter events, 164.5 us)
Async XLA Ops:
  7.2 54.9 %copy-start.1 = (bf16[256,1024]{1,0:T(8,128)(2,1)S(1)}, bf16[256,1024]{1,0:T(8,128)(2,1)}, u32[]{:S(2)}) copy-start(bf16[256,1024]{1,0:T(8,128)(2,1)} %param.16) | copy-start | bytes 1572868
  7.2 58.1 %copy-start.59 = (s32[256,8]{0,1:T(8,128)S(1)}, s32[256,8]{0,1:T(8,128)}, u32[]{:S(2)}) copy-start(s32[256,8]{0,1:T(8,128)} %param.18) | copy-start | bytes 24580
  7.2 58.5 %copy-start.75 = (bf16[256]{0:T(256)(128)(2,1)S(1)}, bf16[256]{0:T(256)(128)(2,1)}, u32[]{:S(2)}) copy-start(bf16[256]{0:T(256)(128)(2,1)} %param.26) | copy-start | bytes 1540
  7.2 28.9 %all-gather.16.cloned.1.call-start = ((), (), s32[]{:S(2)}) async-start(), calls=%async_computation.16 | async-start | bytes 1310720 | tf_op jit(solution)/shard_map/all_gather | solution.py:115
  7.9 54.2 %all-gather.12.cloned.1.call-start = ((), (), s32[]{:S(2)}) async-start(), calls=%async_computation.14 | async-start | bytes 1310720 | tf_op jit(solution)/shard_map/all_gather | solution.py:116
  8.7 76.8 %copy-start.71 = (s32[2]{0:T(128)S(1)}, s32[2]{0:T(128)}, u32[]{:S(2)}) copy-start(s32[2]{0:T(128)} %constant.82) | copy-start | bytes 28
  8.7 76.9 %copy-start.70 = (s32[2]{0:T(128)S(1)}, s32[2]{0:T(128)}, u32[]{:S(2)}) copy-start(s32[2]{0:T(128)} %constant.79) | copy-start | bytes 28
  8.7 86.2 %all-gather.20.cloned.1.call-start = ((), (), s32[]{:S(2)}) async-start(), calls=%async_computation.18 | async-start | bytes 2621440 | tf_op jit(solution)/shard_map/all_gather | solution.py:114
  9.5 113.5 %all-gather.18.cloned.1.call-start = ((), (), s32[]{:S(2)}) async-start(), calls=%async_computation.17 | async-start | bytes 1310720 | tf_op jit(solution)/shard_map/all_gather | solution.py:166
  31.4 66.2 %copy-start.37 = (f32[4,1,256]{2,1,0:T(1,128)}, f32[4,1,256]{2,1,0:T(1,128)S(1)}, u32[]{:S(2)}) copy-start(f32[4,1,256]{2,1,0:T(1,128)S(1)} %convert_element_type.330) | copy-start | bytes 12292
  34.2 63.3 %copy-start.47 = (f32[256]{0:T(256)}, f32[256]{0:T(256)S(1)}, u32[]{:S(2)}) copy-start(f32[256]{0:T(256)S(1)} %fusion.74) | copy-start | bytes 3076
  34.5 64.3 %copy-start.27 = (f32[256,32]{0,1:T(8,128)}, f32[256,32]{0,1:T(8,128)S(1)}, u32[]{:S(2)}) copy-start(f32[256,32]{0,1:T(8,128)S(1)} %get-tuple-element.57) | copy-start | bytes 98308
  34.5 64.3 %copy-start.29 = (f32[256,32]{0,1:T(8,128)}, f32[256,32]{0,1:T(8,128)S(1)}, u32[]{:S(2)}) copy-start(f32[256,32]{0,1:T(8,128)S(1)} %get-tuple-element.58) | copy-start | bytes 98308
  38.2 59.4 %copy-start.41 = (f32[256,8]{0,1:T(8,128)}, f32[256,8]{0,1:T(8,128)S(1)}, u32[]{:S(2)}) copy-start(f32[256,8]{0,1:T(8,128)S(1)} %fusion.71) | copy-start | bytes 24580
  39.9 110.1 %all-gather.14.cloned.1.call-start = ((), (), s32[]{:S(2)}) async-start(), calls=%async_computation.15 | async-start | bytes 1310720 | tf_op jit(solution)/shard_map/all_gather | solution.py:167
  64.6 118.1 %all-gather.22.cloned.1.call-start = ((), (), s32[]{:S(2)}) async-start(), calls=%async_computation.19 | async-start | bytes 2621440 | tf_op jit(solution)/shard_map/all_gather | solution.py:117
  65.7 65.7 %copy-start.62 = (f32[64]{0:T(128)}, f32[64]{0:T(128)S(1)}, u32[]{:S(2)}) copy-start(f32[64]{0:T(128)S(1)} %convert_element_type.265) | copy-start | bytes 772
  65.8 116.9 %copy-start.68 = (pred[256]{0:T(512)(128)(4,1)}, pred[256]{0:T(512)(128)(4,1)S(1)}, u32[]{:S(2)}) copy-start(pred[256]{0:T(512)(128)(4,1)S(1)} %broadcast_compare_fusion.1) | copy-start | bytes 772
  74.7 110.5 %copy-start.45 = (f32[4,1,256]{2,1,0:T(1,128)}, f32[4,1,256]{2,1,0:T(1,128)S(1)}, u32[]{:S(2)}) copy-start(f32[4,1,256]{2,1,0:T(1,128)S(1)} %convert_element_type.331) | copy-start | bytes 12292
  84.0 47.4 %copy-start.18 = (pred[256,1024]{0,1:T(8,128)(4,1)}, pred[256,1024]{0,1:T(8,128)(4,1)S(1)}, u32[]{:S(2)}) copy-start(pred[256,1024]{0,1:T(8,128)(4,1)S(1)} %broadcast_compare_fusion) | copy-start | bytes 786436
  200.0 85.4 %all-to-all-start = ((bf16[32,96,1024]{2,1,0:T(8,128)(2,1)}), bf16[32,96,1024]{2,1,0:T(8,128)(2,1)}, u32[]{:S(2)}, u32[]{:S(2)}) async-start(bf16[32,96,1024]{2,1,0:T(8,128)(2,1)} %bitcast.239), calls=%async_computation | async-start | bytes 12582912 | tf_op jit(solution)/shard_map/all_to_all | solution.py:201
  285.4 88.5 %all-to-all-start.2 = ((bf16[32,96,1024]{2,1,0:T(8,128)(2,1)}), bf16[32,96,1024]{2,1,0:T(8,128)(2,1)}, u32[]{:S(2)}, u32[]{:S(2)}) async-start(bf16[32,96,1024]{2,1,0:T(8,128)(2,1)} %bitcast.238), calls=%async_computation.2 | async-start | bytes 12582912 | tf_op jit(solution)/shard_map/all_to_all | solution.py:229
  290.3 28.4 %all-gather.26.cloned.1.call-start = ((), (), s32[]{:S(2)}) async-start(), calls=%async_computation.21 | async-start | bytes 1310720 | tf_op jit(solution)/shard_map/all_gather | solution.py:210
  291.1 56.2 %all-gather.24.cloned.1.call-start = ((), (), s32[]{:S(2)}) async-start(), calls=%async_computation.20 | async-start | bytes 1310720 | tf_op jit(solution)/shard_map/all_gather | solution.py:209
  291.8 82.1 %all-gather.28.cloned.1.call-start = ((), (), s32[]{:S(2)}) async-start(), calls=%async_computation.22 | async-start | bytes 1310720 | tf_op jit(solution)/shard_map/all_gather | solution.py:211
  486.3 116.0 %all-to-all-start.1 = ((bf16[32,2,49152]{2,1,0:T(2,128)(2,1)}), bf16[32,2,49152]{2,1,0:T(2,128)(2,1)}, u32[]{:S(2)}, u32[]{:S(2)}) async-start(bf16[32,2,49152]{2,1,0:T(2,128)(2,1)} %reshape.554), calls=%async_computation.1 | async-start | bytes 12582912 | tf_op jit(solution)/shard_map/all_to_all | solution.py:218
  602.4 87.8 %all-to-all-start.3 = ((bf16[32,2,49152]{2,1,0:T(2,128)(2,1)}), bf16[32,2,49152]{2,1,0:T(2,128)(2,1)}, u32[]{:S(2)}, u32[]{:S(2)}) async-start(bf16[32,2,49152]{2,1,0:T(2,128)(2,1)} %reshape.556), calls=%async_computation.3 | async-start | bytes 12582912 | tf_op jit(solution)/shard_map/all_to_all | solution.py:266
  610.0 241.2 %reduce-scatter.17.cloned.1.call-start = ((), (), s32[]{:S(2)}) async-start(), calls=%async_computation.24 | async-start | bytes 1310720 | tf_op jit(solution)/shard_map/reduce_scatter | solution.py:326
  690.2 78.0 %copy-start.33 = (f32[256,1,32]{2,1,0:T(1,128)}, f32[256,1,32]{2,1,0:T(1,128)S(1)}, u32[]{:S(2)}) copy-start(f32[256,1,32]{2,1,0:T(1,128)S(1)} %fusion.57) | copy-start | bytes 98308
  721.7 46.6 %copy-start.46 = (f32[4,1,256]{2,1,0:T(1,128)S(1)}, f32[4,1,256]{2,1,0:T(1,128)}, u32[]{:S(2)}) copy-start(f32[4,1,256]{2,1,0:T(1,128)} %copy-done.45) | copy-start | bytes 12292
  721.7 46.6 %copy-start.55 = (f32[256]{0:T(256)S(1)}, f32[256]{0:T(256)}, u32[]{:S(2)}) copy-start(f32[256]{0:T(256)} %copy-done.54) | copy-start | bytes 3076
  781.4 72.4 %reduce-scatter.15.cloned.1.call-start = ((), (), s32[]{:S(2)}) async-start(), calls=%async_computation.23 | async-start | bytes 1310720 | tf_op jit(solution)/shard_map/reduce_scatter | solution.py:320
  814.0 79.2 %reduce-scatter.31.cloned.1.call-start = ((), (), s32[]{:S(2)}) async-start(), calls=%async_computation.31 | async-start | bytes 1310720
  828.4 68.8 %reduce-scatter.33.cloned.1.call-start = ((), (), s32[]{:S(2)}) async-start(), calls=%async_computation.32 | async-start | bytes 1310720
  842.8 72.1 %reduce-scatter.29.cloned.1.call-start = ((), (), s32[]{:S(2)}) async-start(), calls=%async_computation.30 | async-start | bytes 1310720 | tf_op jit(solution)/shard_map/reduce_scatter | solution.py:262
  851.1 89.9 %reduce-scatter.23.cloned.1.call-start = ((), (), s32[]{:S(2)}) async-start(), calls=%async_computation.27 | async-start | bytes 1310720 | tf_op jit(solution)/shard_map/reduce_scatter | solution.py:366
  853.8 113.4 %reduce-scatter.21.cloned.1.call-start = ((), (), s32[]{:S(2)}) async-start(), calls=%async_computation.26 | async-start | bytes 1310720 | tf_op jit(solution)/shard_map/reduce_scatter | solution.py:363
  857.4 141.5 %reduce-scatter.25.cloned.1.call-start = ((), (), s32[]{:S(2)}) async-start(), calls=%async_computation.28 | async-start | bytes 2621440 | tf_op jit(solution)/shard_map/reduce_scatter | solution.py:369
  860.7 169.9 %reduce-scatter.19.cloned.1.call-start = ((), (), s32[]{:S(2)}) async-start(), calls=%async_computation.25 | async-start | bytes 2621440 | tf_op jit(solution)/shard_map/reduce_scatter | solution.py:360
  891.7 162.0 %reduce-scatter.27.cloned.1.call-start = ((), (), s32[]{:S(2)}) async-start(), calls=%async_computation.29 | async-start | bytes 81920 | tf_op jit(solution)/shard_map/reduce_scatter | solution.py:372
  897.2 133.5 %copy-start.40 = (f32[4,1,256]{2,1,0:T(1,128)S(1)}, f32[4,1,256]{2,1,0:T(1,128)}, u32[]{:S(2)}) copy-start(f32[4,1,256]{2,1,0:T(1,128)} %copy-done.37) | copy-start | bytes 12292
  897.2 133.5 %copy-start.50 = (f32[256]{0:T(256)S(1)}, f32[256]{0:T(256)}, u32[]{:S(2)}) copy-start(f32[256]{0:T(256)} %copy-done.47) | copy-start | bytes 3076
  917.7 113.0 %copy-start.26 = (bf16[256,512]{0,1:T(8,128)(2,1)S(1)}, bf16[256,512]{0,1:T(8,128)(2,1)}, u32[]{:S(2)}) copy-start(bf16[256,512]{0,1:T(8,128)(2,1)} %reduce-scatter.17.cloned.1.call-done) | copy-start | bytes 786436
  917.7 115.8 %copy-start.58 = (bf16[1024]{0:T(1024)(128)(2,1)S(1)}, bf16[1024]{0:T(1024)(128)(2,1)}, u32[]{:S(2)}) copy-start(bf16[1024]{0:T(1024)(128)(2,1)} %get-tuple-element.16) | copy-start | bytes 6148
  917.7 115.8 %copy-start.66 = (bf16[64]{0:T(256)(128)(2,1)S(1)}, bf16[64]{0:T(256)(128)(2,1)}, u32[]{:S(2)}) copy-start(bf16[64]{0:T(256)(128)(2,1)} %get-tuple-element.22) | copy-start | bytes 388
  917.7 115.8 %copy-start.67 = (bf16[64]{0:T(256)(128)(2,1)S(1)}, bf16[64]{0:T(256)(128)(2,1)}, u32[]{:S(2)}) copy-start(bf16[64]{0:T(256)(128)(2,1)} %get-tuple-element.20) | copy-start | bytes 388
  917.7 264.9 %copy-start.57 = (f32[256]{0:T(256)S(1)}, f32[256]{0:T(256)}, u32[]{:S(2)}) copy-start(f32[256]{0:T(256)} %copy-done.56) | copy-start | bytes 3076
  917.7 267.4 %all-reduce.16.cloned.1.call-start = ((), (), s32[]{:S(2)}) async-start(), calls=%async_computation.33 | async-start | bytes 3145728 | tf_op jit(solution)/shard_map/psum | solution.py:389
  (54 other events, 785.6 us)
Sparse Core Ops, SparseCore 0:
  9.7 26.3 all-gather.15
  37.8 24.2 all-gather.11
  63.8 31.1 all-gather.19
  97.0 25.8 all-gather.17
  125.0 24.9 all-gather.13
  151.5 31.1 all-gather.21
  292.8 25.9 all-gather.25
  320.4 26.8 all-gather.23
  349.0 24.9 all-gather.27
  781.5 23.8 reduce-scatter.16
  814.1 23.8 reduce-scatter.14
  840.2 23.2 reduce-scatter.30
  866.0 23.2 reduce-scatter.32
  891.6 23.2 reduce-scatter.28
  917.8 23.2 reduce-scatter.22
  943.9 23.2 reduce-scatter.20
  969.6 29.3 reduce-scatter.24
  1001.2 29.3 reduce-scatter.18
  1033.7 19.9 reduce-scatter.26
  1057.2 106.5 all-reduce.15
where the time goes:
time: 1210 us; the launch traced here: 1200 us
  waiting for transfers between devices  341 us (28%)
  local copies, waits for them, and re-layouts  300 us (25%)
  matrix products  188 us (16%)
  blocking collectives  173 us (14%)
  other arithmetic  151 us (12%)
  starting transfers between devices  29 us (2%)
  between operations  18 us (1%)
    unnamed x184, local copies, waits for them, and re-layouts  130 us
    psum x1, blocking collectives, body(): lax.psum(part_first.astype(jnp.bfloat16), 'expert').astype(jnp.float32)  126 us
    unnamed x6, other arithmetic  90.4 us
    all_to_all x1, waiting for transfers between devices, body(): lax.all_to_all(pack_rows(route_rows, flat_experts, slots, experts, CAP),...  48.9 us
    convert_element_type x1, local copies, waits for them, and re-layouts, body(): expert_rows = jnp.einsum('erf,efd->erd', act_low, down_full, preferred_el...  42.6 us
    convert_element_type x1, local copies, waits for them, and re-layouts, body(): grad_inputs = (jnp.einsum('erf,edf->erd', grad_gate_low, gate_full, prefe...  42.6 us
    gather x1, local copies, waits for them, and re-layouts, body(): grad_back[flat_experts, slots].reshape(row_count, topk, width)  40.8 us
    gather x1, local copies, waits for them, and re-layouts, body(): returned[flat_experts, slots].reshape(row_count, topk, width)  40.7 us
  transfers between devices with their start and end apart: 24, of which 16 were waited for; matrix products, arithmetic and copies ran while one was open for 34% of the time, Pallas kernels for 0%

commit v1 on v0

v1 whole, which is shorter than its diff:
```python
import math

import jax
import jax.numpy as jnp
from jax import lax
from jax.experimental import pallas as pl
from jax.experimental.pallas import tpu as pltpu
from jax.sharding import PartitionSpec as P

CAP = 96
EPS = 1e-06
ROPE_BASE = 10000.0
BF = jnp.bfloat16
F32 = jnp.float32
MESH = pl.DeviceIdType.MESH
ANY = pl.BlockSpec(memory_space=pl.ANY)
VMEM = pl.BlockSpec(memory_space=pltpu.VMEM)
MIB = 1 << 20
W_COLS = 3328
W_HALF = W_COLS // 2
ROWS = 256
BLOCK = 272
HALF = 128


class Place:
    def __init__(self):
        self.expert = lax.axis_index("expert")
        self.x = lax.axis_index("shard")
        self.core = self.expert % 2
        self.chip = self.expert // 2
        y, z = self.chip % 4, self.chip // 4
        self.first = z + self.core * (y - z)
        self.second = y + self.core * (z - y)
        self.first_stride = 8 - 6 * self.core
        self.second_stride = 2 + 6 * self.core

    def block(self, first, second):
        return ((self.first + first + 4) % 4) * 4 + (self.second + second + 4) % 4

    def at(self, first, second):
        near = ((self.first + first + 4) % 4) * self.first_stride
        return {"expert": near + ((self.second + second + 4) % 4) * self.second_stride + self.core}

    def along_x(self, step):
        return {"shard": (self.x + step + 4) % 4}

    def sibling(self):
        return {"expert": self.expert + 1 - 2 * self.core}


def greet(devices):
    barrier = pltpu.get_barrier_semaphore()
    for device in devices:
        pl.semaphore_signal(barrier, inc=1, device_id=device, device_id_type=MESH)
    pl.semaphore_wait(barrier, len(devices))


class Copy:
    def __init__(self, *parts):
        self.parts = parts

    def made(self):
        return pltpu.make_async_remote_copy(*self.parts, device_id_type=MESH)

    def start(self):
        self.made().start()

    def wait_send(self):
        self.made().wait_send()

    def wait_recv(self):
        self.made().wait_recv()


class Wires:
    def __init__(self, send, recv):
        self.send, self.recv = send, recv

    def copy(self, source, target, number, device):
        return Copy(source, target, self.send.at[number], self.recv.at[number], device)


class GatherRing:
    def __init__(self, wires, base, at, own, right, left, half, rows):
        low, high, full = pl.ds(0, half), pl.ds(half, rows - half), pl.ds(0, rows)
        copy = wires.copy
        self.go = [copy(own, at(0, full), base, right), copy(own, at(0, full), base + 1, left)]
        self.came = [copy(at(-1, full), at(-1, full), base, right), copy(at(1, full), at(1, full), base + 1, left)]
        self.on = [copy(at(-1, low), at(-1, low), base + 2, right), copy(at(1, high), at(1, high), base + 3, left)]
        self.far = [copy(at(2, low), at(2, low), base + 2, right), copy(at(2, high), at(2, high), base + 3, left)]

    def start(self):
        for step in self.go:
            step.start()

    def forward(self, way):
        self.came[way].wait_recv()
        self.on[way].start()

    def wait_far(self):
        for step in self.far:
            step.wait_recv()

    def wait_sent(self):
        for step in self.go + self.on:
            step.wait_send()


class ReduceRing:
    def __init__(self, wires, base, at, near, landing, right, left, half, rows):
        low, high, full = pl.ds(0, half), pl.ds(half, rows - half), pl.ds(0, rows)
        copy = wires.copy
        self.at, self.near, self.landing = at, near, landing
        self.parts = [low, high, full]
        self.far = [copy(at(2, low), near(low), base, right), copy(at(2, high), near(high), base + 1, left)]
        self.mid = [copy(at(1, full), landing(0), base + 2, right), copy(at(-1, full), landing(1), base + 3, left)]

    def start(self):
        for step in self.far:
            step.start()

    def middle(self, way):
        self.far[way].wait_recv()
        side = 1 - 2 * way
        add_into(self.at(side, self.parts[way]), self.near(self.parts[way]))
        self.mid[way].start()

    def finish(self):
        for step in self.mid:
            step.wait_recv()
        add_into(self.at(0, self.parts[2]), self.landing(0), self.landing(1))

    def wait_sent(self):
        for step in self.far + self.mid:
            step.wait_send()


def add_into(target, *terms):
    rows = target.shape[0]

    @pl.loop(0, rows // 16)
    def _(i):
        here = pl.ds(pl.multiple_of(i * 16, 16), 16)
        total = target[here, :].astype(F32)
        for term in terms:
            total = total + term[here, :].astype(F32)
        target[here, :] = total.astype(target.dtype)


def dot(a, b, contract=((1,), (0,))):
    return lax.dot_general(a, b, (contract, ((), ())), preferred_element_type=F32)


NT = ((1,), (1,))
TN = ((0,), (0,))


def call(kernel, out_shape, in_specs, out_specs, scratch, ident, vmem=56):
    return pl.pallas_call(
        kernel,
        out_shape=out_shape,
        in_specs=in_specs,
        out_specs=out_specs,
        scratch_shapes=scratch,
        compiler_params=pltpu.CompilerParams(
            collective_id=ident, has_side_effects=True, vmem_limit_bytes=vmem * MIB
        ),
    )


def gather_kernel(
    wall, wg, wu, wd, g, wall_full, wg_full, wu_full, wd_full, g_all, local, w_send, w_recv, e_send, e_recv, g_send, g_recv
):
    me = Place()
    x, core = me.x, me.core
    right, left, sibling = me.along_x(1), me.along_x(-1), me.sibling()
    greet([right, left, sibling, me.at(1, 0), me.at(-1, 0), me.at(0, 1), me.at(0, -1)])
    w_wires, e_wires, g_wires = Wires(w_send, w_recv), Wires(e_send, e_recv), Wires(g_send, g_recv)
    cols = pl.ds(pl.multiple_of(core * W_HALF, 128), W_HALF)

    def shard(step):
        return (x + step + 4) % 4

    def w_at(k, rows):
        return wall_full.at[shard(k), rows, cols]

    def slice_of(k):
        return pl.ds(pl.multiple_of(shard(k) * 128, 128), 128)

    w_ring = GatherRing(w_wires, 0, w_at, wall.at[:, cols], right, left, HALF, ROWS)
    w_ring.start()
    first = GatherRing(
        g_wires, 0, lambda k, rows: g_all.at[me.block(k, 0), rows], g, me.at(1, 0), me.at(-1, 0), HALF, BLOCK
    )
    first.start()

    def second(fo, base, own=None):
        own = g_all.at[me.block(fo, 0)] if own is None else own
        return GatherRing(
            g_wires, base, lambda k, rows: g_all.at[me.block(fo, k), rows], own, me.at(0, 1), me.at(0, -1), HALF, BLOCK
        )

    seconds = [second(0, 4, g), second(-1, 8), second(1, 12), second(2, 16)]
    seconds[0].start()
    own_copies = [
        pltpu.make_async_copy(wall, wall_full.at[x], local.at[0]),
        pltpu.make_async_copy(wg, wg_full.at[core, :, slice_of(0)], local.at[1]),
        pltpu.make_async_copy(wu, wu_full.at[core, :, slice_of(0)], local.at[2]),
        pltpu.make_async_copy(wd, wd_full.at[core, slice_of(0), :], local.at[3]),
        pltpu.make_async_copy(g, g_all.at[me.block(0, 0)], local.at[4]),
    ]
    for step in own_copies:
        step.start()

    def g_at(k):
        return wg_full.at[core, :, slice_of(k)]

    def u_at(k):
        return wu_full.at[core, :, slice_of(k)]

    def d_at(k, start=0, size=128):
        return wd_full.at[core, pl.ds(pl.multiple_of(shard(k) * 128 + start, 64), size), :]

    def e_copy(ref, number, device, own=None):
        return e_wires.copy(ref if own is None else own, ref, number, device)

    e_go = [
        e_copy(at(0), way * 3 + i, device, own)
        for way, device in enumerate((right, left))
        for i, (at, own) in enumerate(((g_at, wg), (u_at, wu), (d_at, wd)))
    ]
    e_came = [e_copy(at(side), way * 3 + i, right) for way, side in enumerate((-1, 1)) for i, at in enumerate((g_at, u_at, d_at))]
    e_on = [
        e_copy(g_at(-1), 6, right),
        e_copy(d_at(-1, 0, 64), 7, right),
        e_copy(u_at(1), 8, left),
        e_copy(d_at(1, 64, 64), 9, left),
    ]
    e_far = [e_copy(g_at(2), 6, right), e_copy(d_at(2, 0, 64), 7, right), e_copy(u_at(2), 8, left), e_copy(d_at(2, 64, 64), 9, left)]
    e_pair = [e_copy(ref.at[core], 10 + i, sibling) for i, ref in enumerate((wg_full, wu_full, wd_full))]
    e_pair_came = [e_copy(ref.at[1 - core], 10 + i, sibling) for i, ref in enumerate((wg_full, wu_full, wd_full))]

    other = pl.ds(pl.multiple_of((1 - core) * W_HALF, 128), W_HALF)

    def w_pair(k, number):
        return w_wires.copy(w_at(k, pl.ds(0, ROWS)), w_at(k, pl.ds(0, ROWS)), number, sibling)

    def w_pair_came(k, number):
        ref = wall_full.at[shard(k), :, other]
        return w_wires.copy(ref, ref, number, sibling)

    pairs = [w_pair(-1, 4), w_pair(1, 5), w_pair(2, 6)]
    w_ring.forward(0)
    pairs[0].start()
    w_ring.forward(1)
    pairs[1].start()
    for step in e_go:
        step.start()
    first.forward(0)
    seconds[1].start()
    first.forward(1)
    seconds[2].start()
    seconds[0].forward(0)
    seconds[0].forward(1)
    w_ring.wait_far()
    pairs[2].start()
    first.wait_far()
    seconds[3].start()
    for i in range(3):
        e_came[i].wait_recv()
    e_on[0].start()
    e_on[1].start()
    for i in range(3, 6):
        e_came[i].wait_recv()
    e_on[2].start()
    e_on[3].start()
    for step in seconds[1:3]:
        step.forward(0)
        step.forward(1)
    for step in e_far:
        step.wait_recv()
    for step in own_copies:
        step.wait()
    for step in e_pair:
        step.start()
    seconds[3].forward(0)
    seconds[3].forward(1)
    for i, k in enumerate((-1, 1, 2)):
        w_pair_came(k, 4 + i).wait_recv()
    for step in e_pair_came:
        step.wait_recv()
    for ring in seconds:
        ring.wait_far()
    for ring in [w_ring, first] + seconds:
        ring.wait_sent()
    for step in pairs + e_go + e_on + e_pair:
        step.wait_send()


def gather_all(wall, wg, wu, wd, g):
    dma = pltpu.SemaphoreType.DMA
    return call(
        gather_kernel,
        (
            jax.ShapeDtypeStruct((4, ROWS, W_COLS), BF),
            jax.ShapeDtypeStruct((2, 1024, 512), BF),
            jax.ShapeDtypeStruct((2, 1024, 512), BF),
            jax.ShapeDtypeStruct((2, 512, 1024), BF),
            jax.ShapeDtypeStruct((16, BLOCK, 1024), BF),
        ),
        [ANY] * 5,
        (ANY,) * 5,
        [dma((5,)), dma((7,)), dma((7,)), dma((13,)), dma((13,)), dma((20,)), dma((20,))],
        0,
        vmem=16,
    )(wall, wg, wu, wd, g)


def expert_kernel(
    h_ref,
    g_ref,
    wg,
    wu,
    wd,
    wr,
    dx_out,
    y_out,
    gw_out,
    uw_out,
    dw_out,
    buf,
    gbuf,
    acc_g,
    acc_u,
    acc_d,
    near,
    landing,
    near_f,
    landing_f,
    xb,
    gxb,
    yb,
    act,
    dgb,
    dub,
    hot,
    weight,
    dgate,
    ystage,
    a_send,
    a_recv,
    r_send,
    r_recv,
    local,
    g_local,
    y_local,
):
    me = Place()
    f_right, f_left, s_right, s_left = me.at(1, 0), me.at(-1, 0), me.at(0, 1), me.at(0, -1)
    greet([f_right, f_left, s_right, s_left])
    a_wires, r_wires = Wires(a_send, a_recv), Wires(r_send, r_recv)
    own = buf.at[me.block(0, 0), pl.ds(0, ROWS)]
    fetch = pltpu.make_async_copy(h_ref, own, local.at[0])
    fetch.start()

    def order(i):
        return (3 * i + (i // 2) * (3 + 2 * (i % 2))) % 4

    first = GatherRing(
        a_wires, 0, lambda k, rows: buf.at[me.block(k, 0), rows], own, f_right, f_left, HALF, ROWS
    )

    def second(i):
        fo = order(i)

        def at(k, rows):
            return buf.at[me.block(fo, k), rows]

        return GatherRing(a_wires, 4 + 4 * i, at, at(0, pl.ds(0, ROWS)), s_right, s_left, HALF, ROWS)

    def reduce_second(i):
        fo = order(i)
        return ReduceRing(
            r_wires,
            4 + 4 * i,
            lambda k, rows: buf.at[me.block(fo, k), rows],
            lambda rows: near.at[i, rows],
            lambda way: landing.at[i, way],
            s_right,
            s_left,
            HALF,
            BLOCK,
        )

    reduce_first = ReduceRing(
        r_wires,
        0,
        lambda k, rows: buf.at[me.block(k, 0), rows],
        lambda rows: near_f.at[rows],
        lambda way: landing_f.at[way],
        f_right,
        f_left,
        HALF,
        BLOCK,
    )

    def load_g(i):
        start = ((me.first + order(i)) % 4) * 4
        return pltpu.make_async_copy(g_ref.at[pl.ds(start, 4)], gbuf.at[i % 2], g_local.at[i % 2])

    def store_y(i, j):
        return pltpu.make_async_copy(ystage.at[j], y_out.at[((me.first + order(i)) % 4) * 4 + j], y_local.at[j])

    fetch.wait()
    first.start()
    second(0).start()
    load_g(0).start()
    for acc in (acc_g, acc_u, acc_d):

        @pl.loop(0, acc.shape[1] // 32)
        def _(r):
            acc[:, pl.ds(pl.multiple_of(r * 32, 32), 32), :] = jnp.zeros((2, 32, acc.shape[2]), F32)

    first.forward(0)
    second(1).start()
    first.forward(1)
    second(2).start()
    second(0).forward(0)
    second(0).forward(1)
    first.wait_far()
    second(3).start()

    expert_row = lax.broadcasted_iota(jnp.int32, (32, 256), 0)
    slot_row = lax.broadcasted_iota(jnp.int32, (CAP, 256), 0).astype(F32)
    low_row = lax.broadcasted_iota(jnp.int32, (8, 1024), 0)
    quarter = lax.broadcasted_iota(jnp.int32, (8, 1024), 1) // 256
    my_quarter = quarter == me.chip // 4
    my_low = 2 * (me.chip % 4)

    def pick(table, e):
        return jnp.sum(jnp.where(expert_row == 2 * me.chip + e, table, 0.0), axis=0, keepdims=True)

    @pl.loop(0, 4)
    def _(i):
        base = ((me.first + order(i)) % 4) * 4
        slot = i % 2
        second(i).wait_far()

        @pl.when(i < 3)
        def _():
            load_g(i + 1).start()

        load_g(i).wait()

        @pl.loop(0, 4)
        def _(j):
            h = buf[base + j, pl.ds(0, ROWS), :]
            g = gbuf[slot, j, pl.ds(0, ROWS), :]
            packed = gbuf[slot, j, pl.ds(ROWS, 16), :].astype(F32)[0:8]
            places = jnp.concatenate([packed[:, q * 256 : (q + 1) * 256] for q in range(4)], axis=0)
            logits = dot(wr[...], h, NT)
            routed = places >= 0.0
            top = jnp.max(jnp.where(routed, logits, -1e30), axis=0, keepdims=True)
            terms = jnp.where(routed, jnp.exp(jnp.where(routed, logits - top, 0.0)), 0.0)
            gates = terms / jnp.sum(terms, axis=0, keepdims=True)
            for e in range(2):
                hit = pick(places, e) == slot_row
                rows = pl.ds(e * CAP, CAP)
                weight[j, rows, :] = jnp.sum(jnp.where(hit, pick(gates, e), 0.0), axis=1, keepdims=True)
                hot[j, rows, :] = hit.astype(F32).astype(BF)
            xb[j] = dot(hot[j], h).astype(BF)
            gx = dot(hot[j], g)
            gxb[j] = gx.astype(BF)

        @pl.when(i < 3)
        def _():
            second(i + 1).forward(0)
            second(i + 1).forward(1)

        @pl.loop(0, 2)
        def _(e):
            rows = pl.ds(pl.multiple_of(e * CAP, 32), CAP)
            x = xb[:, rows, :].reshape(4 * CAP, 1024)
            gx = gxb[:, rows, :].reshape(4 * CAP, 1024)
            gate = weight[:, rows, :].reshape(4 * CAP, 1)
            dy = (gate * gx.astype(F32)).astype(BF)
            gate_pre = dot(x, wg[e])
            up_pre = dot(x, wu[e])
            grad_act = dot(dy, wd[e], NT)
            sig = 1.0 / (1.0 + jnp.exp(-gate_pre))
            silu = gate_pre * sig
            active = (silu * up_pre).astype(BF)
            grad_gate = (grad_act * up_pre * (sig * (1.0 + gate_pre * (1.0 - sig)))).astype(BF)
            grad_up = (grad_act * silu).astype(BF)
            act[:, rows, :] = active.reshape(4, CAP, 512)
            dgb[:, rows, :] = grad_gate.reshape(4, CAP, 512)
            dub[:, rows, :] = grad_up.reshape(4, CAP, 512)
            out = dot(active, wd[e]).astype(BF).astype(F32)
            dgate[:, rows, :] = jnp.sum(gx.astype(F32) * out, axis=1, keepdims=True).reshape(4, CAP, 1)
            yb[:, rows, :] = (gate * out).astype(BF).reshape(4, CAP, 1024)

        second(i).wait_sent()

        @pl.when(i == 0)
        def _():
            for step in first.go:
                step.wait_send()

        @pl.when(i == 1)
        def _():
            first.on[0].wait_send()

        @pl.when(i == 2)
        def _():
            first.on[1].wait_send()

        @pl.loop(0, 4)
        def _(j):
            @pl.when(i > 0)
            def _():
                store_y(i - 1, j).wait()

            ystage[j] = dot(hot[j], yb[j], TN).astype(BF)
            store_y(i, j).start()
            spots = hot[j].astype(F32) * dgate[j]
            grad_rows = [jnp.sum(spots[e * CAP : (e + 1) * CAP], axis=0, keepdims=True) for e in range(2)]
            wide = [jnp.concatenate([row] * 4, axis=1) for row in grad_rows]
            mine = jnp.where(low_row == my_low, wide[0], jnp.where(low_row == my_low + 1, wide[1], 0.0))
            mine = jnp.where(my_quarter, mine, 0.0)
            high = mine.astype(BF).astype(F32)
            buf[base + j, pl.ds(ROWS, 16), :] = jnp.concatenate([high, mine - high], axis=0).astype(BF)

        @pl.loop(0, 2)
        def _(e):
            rows = pl.ds(pl.multiple_of(e * CAP, 32), CAP)
            grad_in = dot(dgb[:, rows, :].reshape(4 * CAP, 512), wg[e], NT)
            grad_in = grad_in + dot(dub[:, rows, :].reshape(4 * CAP, 512), wu[e], NT)
            yb[:, rows, :] = grad_in.astype(BF).reshape(4, CAP, 1024)

        @pl.loop(0, 4)
        def _(j):
            buf[base + j, pl.ds(0, ROWS), :] = dot(hot[j], yb[j], TN).astype(BF)

        reduce_second(i).start()

        @pl.when(i > 0)
        def _():
            reduce_second(i - 1).middle(0)
            reduce_second(i - 1).middle(1)

        @pl.loop(0, 2)
        def _(e):
            rows = pl.ds(pl.multiple_of(e * CAP, 32), CAP)
            x = xb[:, rows, :].reshape(4 * CAP, 1024)
            gate = weight[:, rows, :].reshape(4 * CAP, 1)
            dy = (gate * gxb[:, rows, :].reshape(4 * CAP, 1024).astype(F32)).astype(BF)
            grad_gate = dgb[:, rows, :].reshape(4 * CAP, 512)
            grad_up = dub[:, rows, :].reshape(4 * CAP, 512)
            active = act[:, rows, :].reshape(4 * CAP, 512)
            acc_g[e] += dot(x, grad_gate, TN)
            acc_u[e] += dot(x, grad_up, TN)
            acc_d[e] += dot(active, dy, TN)

        @pl.when(i > 1)
        def _():
            reduce_second(i - 2).finish()

    reduce_second(3).middle(0)
    reduce_second(3).middle(1)
    reduce_second(2).finish()
    reduce_second(3).finish()
    reduce_first.start()
    for j in range(4):
        store_y(3, j).wait()

    def stage(slot, width):
        return ystage.at[slot] if width == 1024 else ystage.at[slot, :, pl.ds(0, width)]

    def drain(acc, out):
        width = acc.shape[2]
        blocks = acc.shape[1] // 256

        def leave(n, slot):
            rows = pl.ds(pl.multiple_of((n % blocks) * 256, 256), 256)
            return pltpu.make_async_copy(stage(slot, width), out.at[n // blocks, rows, :], y_local.at[slot])

        @pl.loop(0, 2 * blocks // 4)
        def _(n):
            for slot in range(4):
                number = n * 4 + slot

                @pl.when(n > 0)
                def _():
                    leave(number - 4, slot).wait()

                rows = pl.ds(pl.multiple_of((number % blocks) * 256, 256), 256)
                ystage[slot, :, pl.ds(0, width)] = acc[number // blocks, rows, :].astype(BF)
                leave(number, slot).start()

        for slot in range(4):
            leave(2 * blocks - 4 + slot, slot).wait()

    reduce_first.middle(0)
    reduce_first.middle(1)
    drain(acc_g, gw_out)
    drain(acc_u, uw_out)
    drain(acc_d, dw_out)
    reduce_first.finish()
    dx_out[...] = buf[me.block(0, 0)]
    for step in range(4):
        reduce_second(step).wait_sent()
    reduce_first.wait_sent()


def expert_stage(h, g_all, wg, wu, wd, router):
    dma = pltpu.SemaphoreType.DMA
    return call(
        expert_kernel,
        (
            jax.ShapeDtypeStruct((BLOCK, 1024), BF),
            jax.ShapeDtypeStruct((16, ROWS, 1024), BF),
            jax.ShapeDtypeStruct((2, 1024, 512), BF),
            jax.ShapeDtypeStruct((2, 1024, 512), BF),
            jax.ShapeDtypeStruct((2, 512, 1024), BF),
        ),
        [ANY, ANY, VMEM, VMEM, VMEM, VMEM],
        (VMEM, ANY, ANY, ANY, ANY),
        [
            pltpu.VMEM((16, BLOCK, 1024), BF),
            pltpu.VMEM((2, 4, BLOCK, 1024), BF),
            pltpu.VMEM((2, 1024, 512), F32),
            pltpu.VMEM((2, 1024, 512), F32),
            pltpu.VMEM((2, 512, 1024), F32),
            pltpu.VMEM((4, BLOCK, 1024), BF),
            pltpu.VMEM((4, 2, BLOCK, 1024), BF),
            pltpu.VMEM((BLOCK, 1024), BF),
            pltpu.VMEM((2, BLOCK, 1024), BF),
            pltpu.VMEM((4, 2 * CAP, 1024), BF),
            pltpu.VMEM((4, 2 * CAP, 1024), BF),
            pltpu.VMEM((4, 2 * CAP, 1024), BF),
            pltpu.VMEM((4, 2 * CAP, 512), BF),
            pltpu.VMEM((4, 2 * CAP, 512), BF),
            pltpu.VMEM((4, 2 * CAP, 512), BF),
            pltpu.VMEM((4, 2 * CAP, 256), BF),
            pltpu.VMEM((4, 2 * CAP, 1), F32),
            pltpu.VMEM((4, 2 * CAP, 1), F32),
            pltpu.VMEM((4, ROWS, 1024), BF),
            dma((20,)),
            dma((20,)),
            dma((20,)),
            dma((20,)),
            dma((1,)),
            dma((2,)),
            dma((4,)),
        ],
        1,
        vmem=62,
    )(h, g_all, wg, wu, wd, router)


def reduce_kernel(
    gw,
    uw,
    dw,
    wall,
    y,
    g_out,
    u_out,
    d_out,
    w_out,
    y_out,
    own_g,
    own_u,
    own_d,
    pair_g,
    pair_u,
    pair_d,
    near_g,
    near_u,
    near_d,
    land_g,
    land_u,
    land_d,
    own_w,
    pair_w,
    near_w,
    land_w,
    part_f,
    part_s,
    total_w,
    buf,
    near_s,
    land_s,
    near_f,
    land_f,
    e_send,
    e_recv,
    w_send,
    w_recv,
    p_send,
    p_recv,
    y_send,
    y_recv,
    local,
):
    me = Place()
    x, core = me.x, me.core
    right, left, sibling = me.along_x(1), me.along_x(-1), me.sibling()
    planes = [me.at(1, 0), me.at(-1, 0), me.at(2, 0), me.at(0, 1), me.at(0, -1), me.at(0, 2)]
    greet([right, left, sibling] + planes)
    e_wires, w_wires = Wires(e_send, e_recv), Wires(w_send, w_recv)
    p_wires, y_wires = Wires(p_send, p_recv), Wires(y_send, y_recv)
    cols = pl.ds(pl.multiple_of(core * W_HALF, 128), W_HALF)
    other = pl.ds(pl.multiple_of((1 - core) * W_HALF, 128), W_HALF)

    def shard(step):
        return (x + step + 4) % 4

    pulls = [
        pltpu.make_async_copy(wall.at[:, :, cols], own_w, local.at[0]),
        pltpu.make_async_copy(gw.at[core], own_g, local.at[1]),
        pltpu.make_async_copy(uw.at[core], own_u, local.at[2]),
        pltpu.make_async_copy(dw.at[core], own_d, local.at[3]),
        pltpu.make_async_copy(y, buf, local.at[4]),
    ]
    for step in pulls:
        step.start()
    w_pair = w_wires.copy(wall.at[:, :, other], pair_w, 0, sibling)
    w_pair.start()
    e_pair = [
        e_wires.copy(ref.at[1 - core], land, i, sibling)
        for i, (ref, land) in enumerate(((gw, pair_g), (uw, pair_u), (dw, pair_d)))
    ]
    for step in e_pair:
        step.start()

    def order(i):
        return (3 * i + (i // 2) * (3 + 2 * (i % 2))) % 4

    def y_second(i):
        fo = order(i)
        return ReduceRing(
            y_wires,
            4 + 4 * i,
            lambda k, rows: buf.at[me.block(fo, k), rows],
            lambda rows: near_s.at[i, rows],
            lambda way: land_s.at[i, way],
            me.at(0, 1),
            me.at(0, -1),
            HALF,
            ROWS,
        )

    y_first = ReduceRing(
        y_wires,
        0,
        lambda k, rows: buf.at[me.block(k, 0), rows],
        lambda rows: near_f.at[rows],
        lambda way: land_f.at[way],
        me.at(1, 0),
        me.at(-1, 0),
        HALF,
        ROWS,
    )
    pulls[4].wait()
    y_rings = [y_second(i) for i in range(4)]
    for ring in y_rings:
        ring.start()

    w_ring = ReduceRing(
        w_wires,
        1,
        lambda k, rows: own_w.at[shard(k), rows],
        lambda rows: near_w.at[rows],
        lambda way: land_w.at[way],
        right,
        left,
        HALF,
        ROWS,
    )
    pulls[0].wait()
    w_pair.wait_recv()
    for k in (2, 1, -1, 0):
        add_into(own_w.at[shard(k)], pair_w.at[shard(k)])
        if k == 2:
            w_ring.start()
    for i, (own, land) in enumerate(((own_g, pair_g), (own_u, pair_u), (own_d, pair_d))):
        pulls[1 + i].wait()
        e_pair[i].wait_recv()
        add_into(own, land)

    def slice_of(k):
        return pl.ds(pl.multiple_of(shard(k) * 128, 128), 128)

    def g_at(k):
        return own_g.at[:, slice_of(k)]

    def u_at(k):
        return own_u.at[:, slice_of(k)]

    def d_at(k, start=0, size=128):
        return own_d.at[pl.ds(pl.multiple_of(shard(k) * 128 + start, 64), size), :]

    e_far = [
        e_wires.copy(g_at(2), near_g, 3, right),
        e_wires.copy(d_at(2, 0, 64), near_d.at[0], 4, right),
        e_wires.copy(u_at(2), near_u, 5, left),
        e_wires.copy(d_at(2, 64, 64), near_d.at[1], 6, left),
    ]
    w_ring.middle(0)
    w_ring.middle(1)
    for step in e_far:
        step.start()
    w_ring.finish()

    def piece(base, size, k, at):
        return pl.ds(pl.multiple_of(base + ((at + k + 4) % 4) * size, 16), size)

    mine = own_w.at[x]

    def spread(source, device, land, number):
        return p_wires.copy(source, land, number, device)

    far_f = [
        spread(mine.at[piece(0, 64, k, me.first), :], me.at(k, 0), part_f.at[n], n) for n, k in enumerate((1, 2, 3))
    ]
    for step in far_f:
        step.start()

    e_far[0].wait_recv()
    add_into(g_at(1), near_g)
    e_far[1].wait_recv()
    add_into(d_at(1, 0, 64), near_d.at[0])
    e_mid = [
        e_wires.copy(ref, land.at[way], 7 + way * 3 + i, device)
        for way, (k, device) in enumerate(((1, right), (-1, left)))
        for i, (ref, land) in enumerate(((g_at(k), land_g), (u_at(k), land_u), (d_at(k), land_d)))
    ]
    for step in e_mid[:3]:
        step.start()
    e_far[2].wait_recv()
    add_into(u_at(-1), near_u)
    e_far[3].wait_recv()
    add_into(d_at(-1, 64, 64), near_d.at[1])
    for step in e_mid[3:]:
        step.start()

    for ring in y_rings:
        ring.middle(0)
        ring.middle(1)

    base_f = me.first * 64
    for step in far_f:
        step.wait_recv()
    add_into(mine.at[piece(0, 64, 0, me.first), :], *[part_f.at[n] for n in range(3)])
    far_s = [
        spread(mine.at[piece(base_f, 16, k, me.second), :], me.at(0, k), part_s.at[n], 3 + n)
        for n, k in enumerate((1, 2, 3))
    ]
    for step in far_s:
        step.start()
    for ring in y_rings:
        ring.finish()
    y_first.start()
    for step in far_s:
        step.wait_recv()
    final = piece(base_f, 16, 0, me.second)
    add_into(mine.at[final, :], *[part_s.at[n] for n in range(3)])
    total_w[core, final, :] = mine[final, :]

    def gather(k, number, rows, device):
        here = total_w.at[core, rows]
        return p_wires.copy(here, here, number, device)

    out_s = [gather(k, 6 + n, final, me.at(0, k)) for n, k in enumerate((1, 2, 3))]
    in_s = [gather(k, 6 + n, piece(base_f, 16, -k, me.second), me.at(0, k)) for n, k in enumerate((1, 2, 3))]
    for step in out_s:
        step.start()
    for step in e_mid:
        step.wait_recv()
    for out, at, land in ((g_out, g_at, land_g), (u_out, u_at, land_u), (d_out, d_at, land_d)):

        @pl.loop(0, out.shape[0] // 16)
        def _(i):
            here = pl.ds(pl.multiple_of(i * 16, 16), 16)
            out[here, :] = at(0)[here, :].astype(F32) + land[0, here, :].astype(F32) + land[1, here, :].astype(F32)

    for step in in_s:
        step.wait_recv()
    own_rows = piece(0, 64, 0, me.first)
    out_f = [gather(k, 9 + n, own_rows, me.at(k, 0)) for n, k in enumerate((1, 2, 3))]
    in_f = [gather(k, 9 + n, piece(0, 64, -k, me.first), me.at(k, 0)) for n, k in enumerate((1, 2, 3))]
    for step in out_f:
        step.start()
    y_first.middle(0)
    y_first.middle(1)
    for step in in_f:
        step.wait_recv()
    w_last = w_wires.copy(total_w.at[core], total_w.at[core], 5, sibling)
    w_last.start()
    y_first.finish()
    y_out[...] = buf[me.block(0, 0)]
    w_wires.copy(total_w.at[1 - core], total_w.at[1 - core], 5, sibling).wait_recv()

    @pl.loop(0, ROWS // 16)
    def _(i):
        here = pl.ds(pl.multiple_of(i * 16, 16), 16)
        for half in range(2):
            w_out[here, pl.ds(half * W_HALF, W_HALF)] = total_w[half, here, :].astype(F32)

    for step in [w_pair, w_last] + e_pair + e_far + e_mid + far_f + far_s + out_s + out_f:
        step.wait_send()
    for ring in y_rings + [y_first, w_ring]:
        ring.wait_sent()


def reduce_all(gw, uw, dw, wall, y):
    dma = pltpu.SemaphoreType.DMA
    v = pltpu.VMEM
    return call(
        reduce_kernel,
        (
            jax.ShapeDtypeStruct((1024, 128), F32),
            jax.ShapeDtypeStruct((1024, 128), F32),
            jax.ShapeDtypeStruct((128, 1024), F32),
            jax.ShapeDtypeStruct((ROWS, W_COLS), F32),
            jax.ShapeDtypeStruct((ROWS, 1024), BF),
        ),
        [ANY] * 5,
        (VMEM,) * 5,
        [
            v((1024, 512), BF),
            v((1024, 512), BF),
            v((512, 1024), BF),
            v((1024, 512), BF),
            v((1024, 512), BF),
            v((512, 1024), BF),
            v((1024, 128), BF),
            v((1024, 128), BF),
            v((2, 64, 1024), BF),
            v((2, 1024, 128), BF),
            v((2, 1024, 128), BF),
            v((2, 128, 1024), BF),
            v((4, ROWS, W_HALF), BF),
            v((4, ROWS, W_HALF), BF),
            v((ROWS, W_HALF), BF),
            v((2, ROWS, W_HALF), BF),
            v((3, 64, W_HALF), BF),
            v((3, 16, W_HALF), BF),
            v((2, ROWS, W_HALF), BF),
            v((16, ROWS, 1024), BF),
            v((4, ROWS, 1024), BF),
            v((4, 2, ROWS, 1024), BF),
            v((ROWS, 1024), BF),
            v((2, ROWS, 1024), BF),
            dma((13,)),
            dma((13,)),
            dma((6,)),
            dma((6,)),
            dma((12,)),
            dma((12,)),
            dma((20,)),
            dma((20,)),
            dma((5,)),
        ],
        2,
        vmem=56,
    )(gw, uw, dw, wall, y)


def rms_norm(values, gain):
    inv_rms = lax.rsqrt(jnp.mean(values * values, axis=-1, keepdims=True) + EPS)
    return values * inv_rms * gain


def rope_tables(positions, head_dim):
    half_dim = head_dim // 2
    frequency = ROPE_BASE ** (-(jnp.arange(half_dim, dtype=F32) * (2.0 / head_dim)))
    angles = positions.astype(F32)[:, None] * frequency[None, :]
    return (jnp.cos(angles), jnp.sin(angles))


def rotate(values, cosine, sine_table):
    half_dim = values.shape[-1] // 2
    lower_half = values[..., :half_dim]
    upper_half = values[..., half_dim:]
    cosine = cosine[:, None, :]
    sine_table = sine_table[:, None, :]
    return jnp.concatenate(
        [
            lower_half * cosine - upper_half * sine_table,
            upper_half * cosine + lower_half * sine_table,
        ],
        axis=-1,
    )


def layout(lengths_row, positions):
    doc_ends = jnp.cumsum(lengths_row)
    passed = positions[:, None] >= doc_ends[None, :]
    doc_ids = jnp.sum(passed.astype(jnp.int32), axis=1)
    doc_start = jnp.sum(jnp.where(passed, lengths_row[None, :], 0), axis=1)
    return (doc_ids, positions - doc_start)


def masked_scores(query_low, keys_low, same_doc, kv_heads, head_dim):
    grouped = query_low.reshape(query_low.shape[0], kv_heads, -1, head_dim)
    keyed = keys_low.reshape(keys_low.shape[0], kv_heads, head_dim)
    scores = jnp.einsum("tkgd,skd->kgts", grouped, keyed, preferred_element_type=F32) / math.sqrt(head_dim)
    return jnp.where(same_doc[None, None], scores, -1e30)


def body(
    tokens,
    lengths,
    routes,
    norm1_gain,
    w_query,
    w_key,
    w_value,
    query_gain,
    key_gain,
    w_out,
    norm2_gain,
    w_router,
    w_gate,
    w_up,
    w_down,
    cotangent,
):
    highest = lax.Precision.HIGHEST
    row_count = tokens.shape[0]
    length = row_count * 4
    heads, kv_heads, head_dim, experts, docs = 16, 8, 64, 32, 4
    group = heads // kv_heads
    inv_root = 1.0 / math.sqrt(head_dim)

    hits = jnp.sum((routes[:, :, None] == jnp.arange(experts, dtype=jnp.int32)).astype(F32), axis=1)
    before = (jnp.arange(row_count)[:, None] > jnp.arange(row_count)[None, :]).astype(BF)
    ranks = jnp.dot(before, hits.astype(BF), preferred_element_type=F32)
    hits_t = hits.T
    places = jnp.where(hits_t > 0, ranks.T, -1.0)
    packed = places.reshape(4, 8, row_count).transpose(1, 0, 2).reshape(8, 1024)
    g_block = jnp.concatenate([cotangent, packed.astype(BF), jnp.zeros((8, 1024), BF)], axis=0)

    def column(v):
        return jnp.pad(v.reshape(-1, 1), ((0, row_count - v.shape[0]), (0, 0)))

    extras = jnp.concatenate(
        [w_router, column(norm1_gain), column(norm2_gain), column(query_gain), column(key_gain), jnp.zeros((row_count, 220), BF)],
        axis=1,
    )
    wall = jnp.concatenate([w_query, w_key, w_value, w_out, extras], axis=1)
    wall_full, gate_full, up_full, down_full, g_all = gather_all(wall, w_gate[0], w_up[0], w_down[0], g_block)
    query_full = wall_full[:, :, 0:1024].reshape(1024, 1024)
    key_full = wall_full[:, :, 1024:1536].reshape(1024, 512)
    value_full = wall_full[:, :, 1536:2048].reshape(1024, 512)
    out_full = wall_full[:, :, 2048:3072].reshape(1024, 1024)
    small = wall_full[:, :, 3072:].reshape(1024, 256)
    router_full = small[:, :32]
    gain_first = small[:, 32].astype(F32)
    gain_second = small[:, 33].astype(F32)
    gain_query = small[:, 34].reshape(4, 256)[:, :16].reshape(64).astype(F32)
    gain_key = small[:, 35].reshape(4, 256)[:, :16].reshape(64).astype(F32)

    tokens_float = tokens.astype(F32)
    normed_one, norm_one_back = jax.vjp(rms_norm, tokens_float, gain_first)
    normed_low = normed_one.astype(BF)
    query_pre = jnp.dot(normed_low, query_full, preferred_element_type=F32)
    key_pre = jnp.dot(normed_low, key_full, preferred_element_type=F32)
    value_pre = jnp.dot(normed_low, value_full, preferred_element_type=F32)
    positions = lax.axis_index("shard") * row_count + jnp.arange(row_count, dtype=jnp.int32)
    doc_query, rope_pos = layout(lengths[0], positions)
    doc_key = layout(lengths[0], jnp.arange(length, dtype=jnp.int32))[0]
    cosine, sine_table = rope_tables(rope_pos, head_dim)

    def shape_heads(query_in, key_in, gain_q, gain_k):
        query_rot = rotate(rms_norm(query_in.reshape(row_count, heads, head_dim), gain_q), cosine, sine_table)
        key_rot = rotate(rms_norm(key_in.reshape(row_count, kv_heads, head_dim), gain_k), cosine, sine_table)
        return (query_rot.reshape(row_count, heads * head_dim), key_rot.reshape(row_count, kv_heads * head_dim))

    (query_rot, key_rot), heads_back = jax.vjp(shape_heads, query_pre, key_pre, gain_query, gain_key)
    query_low = query_rot.astype(BF)
    key_low = key_rot.astype(BF)
    value_low = value_pre.astype(BF)
    keys_all, values_all = (
        lax.all_gather(key_low, "shard", axis=0, tiled=True),
        lax.all_gather(value_low, "shard", axis=0, tiled=True),
    )
    same_doc = doc_query[:, None] == doc_key[None, :]
    live_rows = (doc_query < docs)[:, None]
    scores = masked_scores(query_low, keys_all, same_doc, kv_heads, head_dim)
    top_score = jnp.max(scores, axis=-1, keepdims=True)
    exponent_terms = jnp.exp(scores - top_score)
    denominator = jnp.sum(exponent_terms, axis=-1, keepdims=True)
    probs_low = (exponent_terms / denominator).astype(BF)
    log_total = top_score + jnp.log(denominator)
    attn_mixed = jnp.einsum(
        "kgts,skd->tkgd",
        probs_low,
        values_all.reshape(length, kv_heads, head_dim),
        preferred_element_type=F32,
    ).reshape(row_count, heads * head_dim)
    mixed_low = jnp.where(live_rows, attn_mixed, 0.0).astype(BF)
    middle = tokens_float + jnp.dot(mixed_low, out_full, preferred_element_type=F32)
    normed_two, norm_two_back = jax.vjp(rms_norm, middle, gain_second)
    routed_low = normed_two.astype(BF)

    logits = lax.dot_general(router_full, routed_low, (((0,), (1,)), ((), ())), preferred_element_type=F32)
    used = hits_t > 0
    top = jnp.max(jnp.where(used, logits, -1e30), axis=0, keepdims=True)
    terms = jnp.where(used, jnp.exp(jnp.where(used, logits - top, 0.0)), 0.0)
    gates = terms / jnp.sum(terms, axis=0, keepdims=True)

    summed, y_part, gw, uw, dw = expert_stage(routed_low, g_all, gate_full, up_full, down_full, router_full.T)

    grad_result = cotangent.astype(F32)
    grad_routed = summed[:row_count].astype(F32)
    grad_gates = summed[row_count:].astype(F32)
    grad_gates = (grad_gates[:8] + grad_gates[8:]).reshape(8, 4, row_count).transpose(1, 0, 2).reshape(experts, row_count)
    grad_logits = gates * (grad_gates - jnp.sum(gates * grad_gates, axis=0, keepdims=True))
    grad_router = lax.dot_general(
        routed_low.astype(F32), grad_logits, (((0,), (1,)), ((), ())), precision=highest, preferred_element_type=F32
    )
    grad_routed = grad_routed + lax.dot_general(
        grad_logits, router_full.astype(F32), (((0,), (1,)), ((), ())), precision=highest, preferred_element_type=F32
    )
    grad_middle_norm, grad_gain_second = norm_two_back(grad_routed)
    grad_middle = grad_result + grad_middle_norm
    grad_attn_low = grad_middle.astype(BF)
    grad_out_w = jnp.dot(mixed_low.T, grad_attn_low, preferred_element_type=F32)
    grad_mixed = jnp.dot(grad_attn_low, out_full.T, preferred_element_type=F32)
    grad_mixed_low = jnp.where(live_rows, grad_mixed.astype(BF), jnp.zeros((), BF))
    scores_again = masked_scores(query_low, keys_all, same_doc, kv_heads, head_dim)
    attn_probs = jnp.exp(scores_again - log_total)
    grad_heads = grad_mixed_low.reshape(row_count, kv_heads, group, head_dim)
    keys_grouped = keys_all.reshape(length, kv_heads, head_dim)
    values_grouped = values_all.reshape(length, kv_heads, head_dim)
    query_grouped = query_low.reshape(row_count, kv_heads, group, head_dim)
    grad_probs = jnp.einsum("tkgd,skd->kgts", grad_heads, values_grouped, preferred_element_type=F32)
    row_dot = jnp.sum(attn_probs * grad_probs, axis=-1, keepdims=True)
    grad_scores = jnp.where(same_doc[None, None], attn_probs * (grad_probs - row_dot), 0.0).astype(BF)
    grad_values = jnp.einsum("kgts,tkgd->skd", attn_probs.astype(BF), grad_heads, preferred_element_type=F32)
    grad_keys = jnp.einsum("kgts,tkgd->skd", grad_scores, query_grouped, preferred_element_type=F32) * inv_root
    grad_query = jnp.einsum("kgts,skd->tkgd", grad_scores, keys_grouped, preferred_element_type=F32) * inv_root
    own_keys, own_values = (
        lax.psum_scatter(
            grad_keys.reshape(length, kv_heads * head_dim).astype(BF), "shard", scatter_dimension=0, tiled=True
        ).astype(F32),
        lax.psum_scatter(
            grad_values.reshape(length, kv_heads * head_dim).astype(BF), "shard", scatter_dimension=0, tiled=True
        ).astype(F32),
    )
    grad_query_pre, grad_key_pre, grad_gain_query, grad_gain_key = heads_back(
        (grad_query.reshape(row_count, heads * head_dim), own_keys)
    )
    query_grad_low = grad_query_pre.astype(BF)
    key_grad_low = grad_key_pre.astype(BF)
    value_grad_low = own_values.astype(BF)
    grad_query_w = jnp.dot(normed_low.T, query_grad_low, preferred_element_type=F32)
    grad_key_w = jnp.dot(normed_low.T, key_grad_low, preferred_element_type=F32)
    grad_value_w = jnp.dot(normed_low.T, value_grad_low, preferred_element_type=F32)
    grad_normed = (
        jnp.dot(query_grad_low, query_full.T, preferred_element_type=F32)
        + jnp.dot(key_grad_low, key_full.T, preferred_element_type=F32)
        + jnp.dot(value_grad_low, value_full.T, preferred_element_type=F32)
    )
    grad_tokens_norm, grad_gain_first = norm_one_back(grad_normed)
    grad_tokens = grad_middle + grad_tokens_norm

    def spread(v):
        return jnp.pad(v.reshape(4, 16), ((0, 0), (0, row_count - 16))).reshape(1024, 1).astype(BF)

    wall_grad = jnp.concatenate(
        [
            grad_query_w.astype(BF),
            grad_key_w.astype(BF),
            grad_value_w.astype(BF),
            grad_out_w.astype(BF),
            grad_router.astype(BF),
            grad_gain_first.reshape(1024, 1).astype(BF),
            grad_gain_second.reshape(1024, 1).astype(BF),
            spread(grad_gain_query),
            spread(grad_gain_key),
            jnp.zeros((1024, 220), BF),
        ],
        axis=1,
    ).reshape(4, row_count, W_COLS)
    gate_grad, up_grad, down_grad, w_grad, y_sum = reduce_all(gw, uw, dw, wall_grad, y_part)
    result = (middle + y_sum.astype(F32)).astype(BF)
    return (
        result,
        grad_tokens,
        w_grad[:, 3104],
        w_grad[:, 0:1024],
        w_grad[:, 1024:1536],
        w_grad[:, 1536:2048],
        w_grad[:16, 3106],
        w_grad[:16, 3107],
        w_grad[:, 2048:3072],
        w_grad[:, 3105],
        w_grad[:, 3072:3104],
        gate_grad[None],
        up_grad[None],
        down_grad[None],
    )


def solution(mesh):
    rows = P(("expert", "shard"), None)
    by_shard = P("shard", None)
    columns = P("expert", None, "shard")
    placed = (
        rows,
        P("expert", None),
        rows,
        P("shard"),
        by_shard,
        by_shard,
        by_shard,
        P("shard"),
        P("shard"),
        by_shard,
        P("shard"),
        by_shard,
        columns,
        columns,
        P("expert", "shard", None),
        rows,
    )
    return jax.shard_map(
        body,
        mesh=mesh,
        in_specs=placed,
        out_specs=(
            rows,
            rows,
            P("shard"),
            by_shard,
            by_shard,
            by_shard,
            P("shard"),
            P("shard"),
            by_shard,
            P("shard"),
            by_shard,
            columns,
            columns,
            P("expert", "shard", None),
        ),
        check_vma=False,
    )
```

time: 1210 us -> 563 us (0.47)
  waiting for transfers between devices: 341 us -> 23.2 us
  Pallas kernels: 0 us -> 297 us
  local copies, waits for them, and re-layouts: 300 us -> 67 us
  blocking collectives: 173 us -> 0 us
  other arithmetic: 151 us -> 34.2 us
  matrix products: 188 us -> 120 us
  starting transfers between devices: 29 us -> 0.34 us
    pallas_call x0 -> x3, Pallas kernels: none -> 297 us  [the longest x1 128 us: expert_stage(): call(expert_kernel, (jax.ShapeDtypeStruct((BLOCK, 1024), BF), jax.ShapeDt...]
    reduce_scatter x7 -> x1, waiting for transfers between devices: 134 us -> 0.01 us  [body(): lax.psum_scatter(grad_keys.reshape(length, kv_heads * head_dim).astype(BF...]
    psum x1 -> x0, blocking collectives: 126 us -> none  [body(): lax.psum(part_first.astype(jnp.bfloat16), 'expert').astype(jnp.float32)]
    all_gather x7 -> x0, waiting for transfers between devices: 111 us -> none  [the longest x1 26.2 us: body(): lax.all_gather(w_up, 'shard', axis=2, tiled=True)]
    unnamed x184 -> x89, local copies, waits for them, and re-layouts: 130 us -> 22.7 us
    unnamed x6 -> x0, other arithmetic: 90.4 us -> none
    convert_element_type x2 -> x9, local copies, waits for them, and re-layouts: 85.2 us -> 3.71 us  [the longest x4 1.8 us: spread(): jnp.pad(v.reshape(4, 16), ((0, 0), (0, row_count - 16))).reshape(1024, 1)]
    gather x2 -> x0, local copies, waits for them, and re-layouts: 81.5 us -> none  [the longest x1 40.8 us: body(): grad_back[flat_experts, slots].reshape(row_count, topk, width)]
  transfers between devices with their start and end apart: 24 -> 4, of which waited for: 16 -> 3; matrix products, arithmetic and copies ran while one was open for 34% -> 13% of each run, Pallas kernels for 0% -> 0%
where the time goes in v1:
time: 563 us; the launch traced here: 557 us
  Pallas kernels  297 us (53%)
  matrix products  120 us (21%)
  local copies, waits for them, and re-layouts  67 us (12%)
  other arithmetic  34.2 us (6%)
  waiting for transfers between devices  23.2 us (4%)
  between operations  14.6 us (3%)
    pallas_call x1, Pallas kernels, expert_stage(): call(expert_kernel, (jax.ShapeDtypeStruct((BLOCK, 1024), BF), jax.ShapeDt...  128 us
    pallas_call x1, Pallas kernels, reduce_all(): call(reduce_kernel, (jax.ShapeDtypeStruct((1024, 128), F32), jax.ShapeDty...  100 us
    pallas_call x1, Pallas kernels, gather_all(): call(gather_kernel, (jax.ShapeDtypeStruct((4, ROWS, W_COLS), BF), jax.Sha...  69.2 us
    dot_general x1, matrix products, body(): jnp.einsum('kgts,tkgd->skd', grad_scores, query_grouped, preferred_elemen...  24.4 us
    dot_general x1, matrix products, body(): jnp.einsum('kgts,skd->tkgd', grad_scores, keys_grouped, preferred_element...  23.9 us
    unnamed x89, local copies, waits for them, and re-layouts  22.7 us
    concatenate x1, local copies, waits for them, and re-layouts, body(): jnp.concatenate([grad_query_w.astype(BF), grad_key_w.astype(BF), grad_val...  12 us
  transfers between devices with their start and end apart: 4, of which 3 were waited for; matrix products, arithmetic and copies ran while one was open for 13% of the time, Pallas kernels for 0%

profile of v1, /device:TPU:0, one launch (start us, length us, event | category | flops | bytes accessed | tf_op | source)
XLA Modules:
  0.0 557.1 jit_solution(16617307718443597144)
XLA Ops:
  13.4 2.5 concatenate.28.wall
  18.8 69.2 %shard_map.263 = (bf16[4,256,3328]{2,1,0:T(8,128)(2,1)S(1)}, bf16[2,1024,512]{2,1,0:T(8,128)(2,1)S(1)}, bf16[2,1024,512]{2,1,0:T(8,128)(2,1)S(1)}, bf16[2,512,10...) custom-call(bf16[256,3328]{1,0:T(8,128)(2,1)S(1)} %concatenate.28.wall, bf16[1024,128]{1,0:T(8,128)(2,1)S(1)} %bitcast.170, ...), custom_call_target="tpu_custom_call" | custom-call | tf_op jit(solution)/shard_map/pallas_call | solution.py:303
  88.0 3.4 copy-done
  91.5 2.7 copy-done.1
  94.2 1.9 fusion.62
  99.8 1.8 multiply_reduce_fusion.8
  102.9 2.4 convolution_convert_fusion.5
  105.6 4.2 fusion.61
  109.9 2.6 copy.78
  112.5 3.4 multiply_reduce_fusion.5
  116.0 1.4 multiply_multiply_fusion
  121.3 1.7 copy.104
  123.0 4.2 all-gather.5.cloned.1.call-done
  127.2 9.6 %fusion.65 = (f32[8,2,256]{2,1,0:T(2,128)S(1)}, f32[8,2,256,1024]{2,3,1,0:T(8,128)}) fusion(bf16[1024,8,64,1]{0,2,3,1:T(8,128)(2,1)} %bitcast.198, bf16[256,8,2,64]{0,3,2,1:T(8,128)(2,1)} %bitcast.196, pred[256,1024]{0,1:T(8,128)(4,1)S(1)} %broadcast_compare_fusion), kind=kOutput, calls=%fused_computation.152 | convolution fusion | flops 549449728 | bytes 18628608 | tf_op jit(solution)/shard_map/tkgd,skd->kgts/dot_general | solution.py:1010
  136.9 8.3 %fusion.4 = f32[8,2,256]{2,1,0:T(2,128)S(1)} fusion(f32[8,2,256,1024]{2,3,1,0:T(8,128)} %get-tuple-element.127, f32[8,2,256]{2,1,0:T(2,128)S(1)} %get-tuple-element.126), kind=kLoop, calls=%fused_computation.10 | loop fusion | flops 8384512 | bytes 16809984 | tf_op jit(solution)/shard_map/reduce_sum | solution.py:1096
  145.1 9.3 %all-gather.3.cloned.1.call-done = bf16[1024,512]{1,0:T(8,128)(2,1)} async-done(((bf16[256,512]{1,0:T(8,128)(2,1)}), bf16[1024,512]{1,0:T(8,128)(2,1)}) %all-gather.3.cloned.1.call-update) | async-done | bytes 1048592 | tf_op jit(solution)/shard_map/all_gather | solution.py:1089
  154.5 1.5 copy.76
  156.0 8.5 %fusion.28 = (bf16[256,8,2,64]{0,3,2,1:T(8,128)(2,1)S(1)}, bf16[8,64,2,256]{3,1,2,0:T(8,128)(2,1)}) fusion(pred[256]{0:T(512)(128)(4,1)S(1)} %broadcast_compare_fusion.2, bf16[1024,8,64,1]{0,2,3,1:T(8,128)(2,1)S(1)} %bitcast.185, f32[8,2,256,1024]{2,3,1,0:T(8,128)} %get-tuple-element.127, f32[8,2,256]{2,1,0:T(2,128)S(1)} %fusion.4, ...), kind=kOutput, calls=%fused_computation.53 | convolution fusion | flops 549715968 | bytes 18907392 | tf_op jit(solution)/shard_map/kgts,skd->tkgd/dot_general | solution.py:1099
  166.9 127.7 %shard_map.264 = (bf16[272,1024]{1,0:T(8,128)(2,1)}, bf16[16,256,1024]{2,1,0:T(8,128)(2,1)}, bf16[2,1024,512]{2,1,0:T(8,128)(2,1)}, bf16[2,1024,512]{2,1,0:T(8,128)(2,1)}, bf16[2,512,1024]{2,1,0:T(8,128)(2,1)}) custom-call(bf16[256,1024]{1,0:T(8,128)(2,1)} %copy-done.14, bf16[16,272,1024]{2,1,0:T(8,128)(2,1)} %copy-done, bf16[2,1024,512]{2,1,0:T(8,128)(2,1)} %copy-done.2, ...), custom_call_target="tpu_custom_call" | custom-call | tf_op jit(solution)/shard_map/pallas_call | solution.py:618
  295.5 2.1 multiply_reduce_fusion.1
  299.7 3.1 fusion.19
  302.8 2.0 copy.80
  304.8 9.5 %fusion.66 = f32[8,1024,256,2]{2,1,3,0:T(8,128)} fusion(bf16[1024,8,64,1]{0,2,3,1:T(8,128)(2,1)} %bitcast.186, bf16[256,8,2,64]{0,3,2,1:T(8,128)(2,1)} %bitcast.187), kind=kOutput, calls=%fused_computation.153 | convolution fusion | flops 536870912 | bytes 18350080 | tf_op jit(solution)/shard_map/tkgd,skd->kgts/dot_general | solution.py:1141
  314.3 23.9 %fusion.16 = f32[8,64,2,256]{3,1,2,0:T(8,128)} fusion(bf16[1024,8,64,1]{0,2,3,1:T(8,128)(2,1)} %bitcast.199, f32[8,1024,256,2]{2,1,3,0:T(8,128)} %fusion.66, f32[8,2,256,1024]{2,3,1,0:T(8,128)} %get-tuple-element.127, f32[8,2,256]{2,1,0:T(2,128)S(1)} %bitcast.231, pred[256,1024]{0,1:T(8,128)(4,1)S(1)} %broadcast_compare_fusion), kind=kOutput, calls=%fused_computation.36 | convolution fusion | flops 566498304 | bytes 35930112 | tf_op jit(solution)/shard_map/kgts,skd->tkgd/dot_general | solution.py:1146
  338.3 24.4 %fusion.13 = bf16[8,64,1024]{2,1,0:T(8,128)(2,1)} fusion(bf16[256,8,2,64]{0,3,2,1:T(8,128)(2,1)} %bitcast.197, f32[8,1024,256,2]{2,1,3,0:T(8,128)} %fusion.66, f32[8,2,256,1024]{2,3,1,0:T(8,128)} %get-tuple-element.127, f32[8,2,256]{2,1,0:T(2,128)S(1)} %bitcast.232, pred[256,1024]{0,1:T(8,128)(4,1)S(1)} %broadcast_compare_fusion), kind=kOutput, calls=%fused_computation.20 | convolution fusion | flops 567284736 | bytes 35405824 | tf_op jit(solution)/shard_map/kgts,tkgd->skd/dot_general | solution.py:1145
  364.9 1.7 multiply_reduce_fusion
  366.7 1.4 convolution_convert_fusion.6
  368.1 1.8 fusion.24
  370.7 2.2 convolution_convert_fusion.1
  372.9 9.7 %bitcast_convert_fusion = bf16[8,64,1024]{2,1,0:T(8,128)(2,1)} fusion(bf16[256,8,2,64]{0,3,2,1:T(8,128)(2,1)} %bitcast.188, f32[8,2,256,1024]{2,3,1,0:T(8,128)} %get-tuple-element.127, f32[8,2,256]{2,1,0:T(2,128)S(1)} %bitcast.233), kind=kOutput, calls=%fused_computation.18 | convolution fusion | flops 545783808 | bytes 18366464 | tf_op jit(solution)/shard_map/kgts,tkgd->skd/dot_general | solution.py:1144
  382.9 2.0 copy.84
  386.9 3.5 fusion.67
  390.5 3.3 convolution_convert_fusion
  397.4 1.6 convolution_convert_fusion.3
  399.0 3.0 convolution_add_fusion.1
  402.0 9.6 %reduce-scatter.5.cloned.1.call-done = bf16[256,512]{0,1:T(8,128)(2,1)} async-done(((bf16[1024,512]{0,1:T(8,128)(2,1)}), bf16[256,512]{0,1:T(8,128)(2,1)}) %reduce-scatter.5.cloned.1.call-update) | async-done | bytes 262160 | tf_op jit(solution)/shard_map/reduce_scatter | solution.py:1151
  411.5 3.2 fusion.27
  416.2 2.5 convolution_convert_fusion.2
  419.5 12.0 %concatenate.37.wall = bf16[4,256,3328]{2,1,0:T(8,128)(2,1)} concatenate(bf16[4,256,1024]{2,1,0:T(8,128)(2,1)} %bitcast.183, bf16[4,256,512]{2,1,0:T(8,128)(2,1)} %bitcast.191, bf16[4,256,512]{2,1,0:T(8,128)(2,1)} %bitcast.192, bf16[4,256,1024]{2,1,0:T(8,128)(2,1)} %bitcast.184, bf16[4,256,32]{2,1,0:T(8,128)(2,1)S(1)} %bitcast.203, bf16[4,256,1]{2,1,0:T(8,128)(2,1)S(1)} %convert_element_type.294, ...), dimensions={2} | concatenate | bytes 13631488 | tf_op jit(solution)/shard_map/concatenate | solution.py:1175
  431.5 100.4 %shard_map.265 = (f32[1024,128]{1,0:T(8,128)}, f32[1024,128]{1,0:T(8,128)}, f32[128,1024]{1,0:T(8,128)}, f32[256,3328]{1,0:T(8,128)}, bf16[256,1024]{1,0:T(8,128)(2,1)}) custom-call(bf16[2,1024,512]{2,1,0:T(8,128)(2,1)} %get-tuple-element.34.gw, bf16[2,1024,512]{2,1,0:T(8,128)(2,1)} %get-tuple-element.35.uw, bf16[2,512,1024]{2,1,0:T(8,128)(2,1)} %get-tuple-element.36.dw, ...), custom_call_target="tpu_custom_call" | custom-call | tf_op jit(solution)/shard_map/pallas_call | solution.py:921
  531.9 2.2 fusion.64
  535.0 1.8 slice_reduce_fusion.2
  536.8 1.5 slice_reduce_fusion.4
  538.3 3.3 fusion.63
  542.3 2.5 fusion.25
  544.7 1.9 copy.117
  546.6 1.9 copy.118
  548.5 1.9 copy.119
  (162 shorter events, 36.3 us)
Async XLA Ops:
  7.2 90.2 %copy-start.8 = (bf16[256,1024]{1,0:T(8,128)(2,1)S(1)}, bf16[256,1024]{1,0:T(8,128)(2,1)}, u32[]{:S(2)}) copy-start(bf16[256,1024]{1,0:T(8,128)(2,1)} %param.16) | copy-start | bytes 1572868
  7.2 90.5 %copy-start.39 = (s32[1,4]{1,0:T(1,128)S(1)}, s32[1,4]{1,0:T(1,128)}, u32[]{:S(2)}) copy-start(s32[1,4]{1,0:T(1,128)} %param.17) | copy-start | bytes 52
  7.2 120.0 %all-gather.5.cloned.1.call-start = ((), (), s32[]{:S(2)}) async-start(), calls=%async_computation.3 | async-start | bytes 1310720 | tf_op jit(solution)/shard_map/all_gather | solution.py:1088
  16.0 1.0 copy-start.5
  16.9 0.9 copy-start.6
  17.9 0.9 copy-start.7
  88.0 3.4 copy-start
  91.4 2.8 copy-start.1
  91.4 4.7 copy-start.2
  91.4 4.7 copy-start.3
  91.4 5.8 %copy-start.4 = (bf16[2,512,1024]{2,1,0:T(8,128)(2,1)}, bf16[2,512,1024]{2,1,0:T(8,128)(2,1)S(1)}, u32[]{:S(2)}) copy-start(bf16[2,512,1024]{2,1,0:T(8,128)(2,1)S(1)} %get-tuple-element.33.wd) | copy-start | bytes 6291460
  94.2 25.1 %copy-start.11 = (bf16[4,256,256]{2,1,0:T(8,128)(2,1)}, bf16[4,256,256]{2,1,0:T(8,128)(2,1)S(1)}, u32[]{:S(2)}) copy-start(bf16[4,256,256]{2,1,0:T(8,128)(2,1)S(1)} %slice.87) | copy-start | bytes 1572868
  96.1 9.3 %copy-start.13 = (bf16[4,256,512]{2,1,0:T(8,128)(2,1)}, bf16[4,256,512]{2,1,0:T(8,128)(2,1)S(1)}, u32[]{:S(2)}) copy-start(bf16[4,256,512]{2,1,0:T(8,128)(2,1)S(1)} %get-tuple-element.104) | copy-start | bytes 3145732
  97.6 8.0 %copy-start.27 = (f32[256]{0:T(256)}, f32[256]{0:T(256)S(1)}, u32[]{:S(2)}) copy-start(f32[256]{0:T(256)S(1)} %fusion.26) | copy-start | bytes 3076
  97.8 3.8 copy-start.35
  101.6 3.8 copy-start.16
  101.6 10.9 %copy-start.24 = (f32[256,8]{0,1:T(8,128)}, f32[256,8]{0,1:T(8,128)S(1)}, u32[]{:S(2)}) copy-start(f32[256,8]{0,1:T(8,128)S(1)} %get-tuple-element.122) | copy-start | bytes 24580
  101.8 10.7 %copy-start.30 = (f32[64]{0:T(128)}, f32[64]{0:T(128)S(1)}, u32[]{:S(2)}) copy-start(f32[64]{0:T(128)S(1)} %reshape.439) | copy-start | bytes 772
  101.8 8.1 %copy-start.36 = (s32[4,1]{0,1:T(1,128)S(1)}, s32[4,1]{0,1:T(1,128)}, u32[]{:S(2)}) copy-start(s32[4,1]{0,1:T(1,128)} %copy-done.35) | copy-start | bytes 52
  102.9 51.6 %all-gather.3.cloned.1.call-start = ((), (), s32[]{:S(2)}) async-start(), calls=%async_computation.2 | async-start | bytes 1310720 | tf_op jit(solution)/shard_map/all_gather | solution.py:1089
  105.4 12.2 %copy-start.34 = (s32[256]{0:T(256)S(1)}, s32[256]{0:T(256)}, u32[]{:S(2)}) copy-start(s32[256]{0:T(256)} %get-tuple-element.100) | copy-start | bytes 3076
  105.4 288.3 %reduce-scatter.3.cloned.1.call-start = ((), (), s32[]{:S(2)}) async-start(), calls=%async_computation.4 | async-start | bytes 1310720 | tf_op jit(solution)/shard_map/reduce_scatter | solution.py:1148
  109.8 27.0 %copy-start.9 = (bf16[4,256,1024]{2,1,0:T(8,128)(2,1)}, bf16[4,256,1024]{2,1,0:T(8,128)(2,1)S(1)}, u32[]{:S(2)}) copy-start(bf16[4,256,1024]{2,1,0:T(8,128)(2,1)S(1)} %get-tuple-element.103) | copy-start | bytes 6291460
  115.9 1.7 copy-start.20
  116.0 1.6 copy-start.32
  117.6 38.3 %copy-start.37 = (pred[256]{0:T(512)(128)(4,1)}, pred[256]{0:T(512)(128)(4,1)S(1)}, u32[]{:S(2)}) copy-start(pred[256]{0:T(512)(128)(4,1)S(1)} %broadcast_compare_fusion.2) | copy-start | bytes 772
  145.1 19.4 %copy-start.22 = (f32[8,2,256]{2,1,0:T(2,128)}, f32[8,2,256]{2,1,0:T(2,128)S(1)}, u32[]{:S(2)}) copy-start(f32[8,2,256]{2,1,0:T(2,128)S(1)} %fusion.4) | copy-start | bytes 49156
  155.9 8.6 %copy-start.15 = (bf16[1024,512]{0,1:T(8,128)(2,1)}, bf16[1024,512]{0,1:T(8,128)(2,1)S(1)}, u32[]{:S(2)}) copy-start(bf16[1024,512]{0,1:T(8,128)(2,1)S(1)} %copy.76) | copy-start | bytes 3145732
  156.0 8.6 %copy-start.10 = (bf16[4,256,1024]{2,1,0:T(8,128)(2,1)S(1)}, bf16[4,256,1024]{2,1,0:T(8,128)(2,1)}, u32[]{:S(2)}) copy-start(bf16[4,256,1024]{2,1,0:T(8,128)(2,1)} %get-tuple-element.102) | copy-start | bytes 6291460
  156.0 10.1 %copy-start.12 = (bf16[4,256,256]{2,1,0:T(8,128)(2,1)S(1)}, bf16[4,256,256]{2,1,0:T(8,128)(2,1)}, u32[]{:S(2)}) copy-start(bf16[4,256,256]{2,1,0:T(8,128)(2,1)} %copy-done.11) | copy-start | bytes 1572868
  165.4 0.6 copy-start.29
  165.4 0.6 copy-start.26
  166.1 0.8 copy-start.14
  304.8 9.5 %copy-start.23 = (f32[8,2,256]{2,1,0:T(2,128)S(1)}, f32[8,2,256]{2,1,0:T(2,128)}, u32[]{:S(2)}) copy-start(f32[8,2,256]{2,1,0:T(2,128)} %copy-done.22) | copy-start | bytes 49156
  338.2 26.7 %copy-start.33 = (f32[64]{0:T(128)S(1)}, f32[64]{0:T(128)}, u32[]{:S(2)}) copy-start(f32[64]{0:T(128)} %copy-done.32) | copy-start | bytes 772
  338.3 28.4 %copy-start.21 = (f32[256,16]{0,1:T(8,128)S(1)}, f32[256,16]{0,1:T(8,128)}, u32[]{:S(2)}) copy-start(f32[256,16]{0,1:T(8,128)} %copy-done.20) | copy-start | bytes 49156
  362.7 48.8 %reduce-scatter.5.cloned.1.call-start = ((), (), s32[]{:S(2)}) async-start(), calls=%async_computation.5 | async-start | bytes 1310720 | tf_op jit(solution)/shard_map/reduce_scatter | solution.py:1151
  364.1 0.8 copy-start.18
  364.1 2.5 copy-start.19
  369.9 0.8 copy-start.17
  372.9 17.5 %copy-start.38 = (pred[256]{0:T(512)(128)(4,1)S(1)}, pred[256]{0:T(512)(128)(4,1)}, u32[]{:S(2)}) copy-start(pred[256]{0:T(512)(128)(4,1)} %copy-done.37) | copy-start | bytes 772
  382.6 12.2 %copy-start.31 = (f32[64]{0:T(128)S(1)}, f32[64]{0:T(128)}, u32[]{:S(2)}) copy-start(f32[64]{0:T(128)} %copy-done.30) | copy-start | bytes 772
  382.6 13.5 %copy-start.25 = (f32[256,8]{0,1:T(8,128)S(1)}, f32[256,8]{0,1:T(8,128)}, u32[]{:S(2)}) copy-start(f32[256,8]{0,1:T(8,128)} %copy-done.24) | copy-start | bytes 24580
  431.5 106.8 %copy-start.28 = (f32[256]{0:T(256)S(1)}, f32[256]{0:T(256)}, u32[]{:S(2)}) copy-start(f32[256]{0:T(256)} %copy-done.27) | copy-start | bytes 3076
Sparse Core Ops, SparseCore 0:
  103.0 24.1 all-gather.4
  129.5 24.9 all-gather.2
  362.8 22.4 reduce-scatter.2
  388.2 23.2 reduce-scatter.4

commit v2 on v1

v2 whole, which is shorter than its diff:
```python
import math

import jax
import jax.numpy as jnp
import numpy as np
from jax import lax
from jax.experimental import pallas as pl
from jax.experimental.pallas import tpu as pltpu
from jax.sharding import PartitionSpec as P

CAP = 96
EPS = 1e-06
ROPE_BASE = 10000.0
BF = jnp.bfloat16
F32 = jnp.float32
MESH = pl.DeviceIdType.MESH
ANY = pl.BlockSpec(memory_space=pl.ANY)
VMEM = pl.BlockSpec(memory_space=pltpu.VMEM)
MIB = 1 << 20
W_COLS = 3328
W_HALF = W_COLS // 2
ROWS = 256
BLOCK = 272
HALF = 128


class Place:
    def __init__(self):
        self.expert = lax.axis_index("expert")
        self.x = lax.axis_index("shard")
        self.core = self.expert % 2
        self.chip = self.expert // 2
        y, z = self.chip % 4, self.chip // 4
        self.first = z + self.core * (y - z)
        self.second = y + self.core * (z - y)
        self.first_stride = 8 - 6 * self.core
        self.second_stride = 2 + 6 * self.core

    def block(self, first, second):
        return ((self.first + first + 4) % 4) * 4 + (self.second + second + 4) % 4

    def at(self, first, second):
        near = ((self.first + first + 4) % 4) * self.first_stride
        return {"expert": near + ((self.second + second + 4) % 4) * self.second_stride + self.core}

    def along_x(self, step):
        return {"shard": (self.x + step + 4) % 4}

    def sibling(self):
        return {"expert": self.expert + 1 - 2 * self.core}


def greet(devices):
    barrier = pltpu.get_barrier_semaphore()
    for device in devices:
        pl.semaphore_signal(barrier, inc=1, device_id=device, device_id_type=MESH)
    pl.semaphore_wait(barrier, len(devices))


class Copy:
    def __init__(self, *parts):
        self.parts = parts

    def made(self):
        return pltpu.make_async_remote_copy(*self.parts, device_id_type=MESH)

    def start(self):
        self.made().start()

    def wait_send(self):
        self.made().wait_send()

    def wait_recv(self):
        self.made().wait_recv()


class Wires:
    def __init__(self, send, recv):
        self.send, self.recv = send, recv

    def copy(self, source, target, number, device):
        return Copy(source, target, self.send.at[number], self.recv.at[number], device)


class GatherRing:
    def __init__(self, wires, base, at, own, right, left, half, rows):
        low, high, full = pl.ds(0, half), pl.ds(half, rows - half), pl.ds(0, rows)
        copy = wires.copy
        self.go = [copy(own, at(0, full), base, right), copy(own, at(0, full), base + 1, left)]
        self.came = [copy(at(-1, full), at(-1, full), base, right), copy(at(1, full), at(1, full), base + 1, left)]
        self.on = [copy(at(-1, low), at(-1, low), base + 2, right), copy(at(1, high), at(1, high), base + 3, left)]
        self.far = [copy(at(2, low), at(2, low), base + 2, right), copy(at(2, high), at(2, high), base + 3, left)]

    def start(self):
        for step in self.go:
            step.start()

    def forward(self, way):
        self.came[way].wait_recv()
        self.on[way].start()

    def wait_far(self):
        for step in self.far:
            step.wait_recv()

    def wait_sent(self):
        for step in self.go + self.on:
            step.wait_send()


class ReduceRing:
    def __init__(self, wires, base, at, near, landing, right, left, half, rows):
        low, high, full = pl.ds(0, half), pl.ds(half, rows - half), pl.ds(0, rows)
        copy = wires.copy
        self.at, self.near, self.landing = at, near, landing
        self.parts = [low, high, full]
        self.far = [copy(at(2, low), near(low), base, right), copy(at(2, high), near(high), base + 1, left)]
        self.mid = [copy(at(1, full), landing(0), base + 2, right), copy(at(-1, full), landing(1), base + 3, left)]

    def start(self):
        for step in self.far:
            step.start()

    def middle(self, way):
        self.far[way].wait_recv()
        side = 1 - 2 * way
        add_into(self.at(side, self.parts[way]), self.near(self.parts[way]))
        self.mid[way].start()

    def middle_both(self):
        for way in range(2):
            self.far[way].wait_recv()
        for way in range(2):
            add_into(self.at(1 - 2 * way, self.parts[way]), self.near(self.parts[way]))
        for way in range(2):
            self.mid[way].start()

    def finish(self, target=None):
        for step in self.mid:
            step.wait_recv()
        own = self.at(0, self.parts[2])
        if target is None:
            add_into(own, self.landing(0), self.landing(1))
        else:
            add_up(target, own, self.landing(0), self.landing(1))

    def wait_sent(self):
        for step in self.far + self.mid:
            step.wait_send()


def add_up(target, *terms):
    rows, columns = target.shape
    size = min(rows, 16 * max(1, 1024 // columns))

    @pl.loop(0, rows // size)
    def _(i):
        here = pl.ds(pl.multiple_of(i * size, 16), size)
        total = terms[0][here, :].astype(F32)
        for term in terms[1:]:
            total = total + term[here, :].astype(F32)
        target[here, :] = total.astype(target.dtype)


def add_into(target, *terms):
    add_up(target, target, *terms)


def dot(a, b, contract=((1,), (0,))):
    return lax.dot_general(a, b, (contract, ((), ())), preferred_element_type=F32)


NT = ((1,), (1,))
TN = ((0,), (0,))


def call(kernel, out_shape, in_specs, out_specs, scratch, ident, vmem=56):
    return pl.pallas_call(
        kernel,
        out_shape=out_shape,
        in_specs=in_specs,
        out_specs=out_specs,
        scratch_shapes=scratch,
        compiler_params=pltpu.CompilerParams(
            collective_id=ident, has_side_effects=True, vmem_limit_bytes=vmem * MIB
        ),
    )


HEAD_PAIRS = 4
NORM_ROW, QUERY_ROW = 0, 2
ROUTER_ROW = 16
SMALL = 48


def lanes(rows=ROWS, columns=128):
    return lax.broadcasted_iota(jnp.int32, (rows, columns), 1)


def head_map(columns):
    column = lax.broadcasted_iota(jnp.int32, (columns, 128), 0) // 64
    return (column == lax.broadcasted_iota(jnp.int32, (columns, 128), 1)).astype(F32).astype(BF)


def split_dot(a, exact, contract=((1,), (0,))):
    high = a.astype(BF)
    low = (a - high.astype(F32)).astype(BF)
    return dot(high, exact, contract) + dot(low, exact, contract)


def head_scale(v, heads):
    mean = split_dot(v * v, heads) * (1.0 / 64)
    return split_dot(lax.rsqrt(mean + EPS), heads, NT)


def turn(v, cosine, sine):
    lower = lanes() % 64 < 32
    swapped = jnp.where(lower, pltpu.roll(v, 96, 1), pltpu.roll(v, 32, 1))
    return v * cosine + swapped * sine


def split_heads(block, odd):
    keep = lanes() >= 64 if odd else lanes() < 64
    rolled = pltpu.roll(block, 64, 1)
    first, second = (rolled, block) if odd else (block, rolled)
    return jnp.where(keep, first, 0.0), jnp.where(keep, second, 0.0)


def join_heads(first, second, odd):
    low = pltpu.roll(first, 64, 1) if odd else first
    high = second if odd else pltpu.roll(second, 64, 1)
    return jnp.where(lanes() < 64, low, high)


def three_parts(v):
    high = v.astype(BF).astype(F32)
    middle = (v - high).astype(BF).astype(F32)
    return high, middle, v - high - middle


def passed_documents(lengths, rows, first):
    position = (lax.broadcasted_iota(jnp.int32, (rows, 128), 0) + first).astype(F32)
    end = jnp.zeros((1, 1), F32)
    number, start = jnp.zeros((rows, 128), F32), jnp.zeros((rows, 128), F32)
    for d in range(4):
        length = lengths[:, d : d + 1]
        end = end + length
        number = number + jnp.where(position >= end, 1.0, 0.0)
        start = start + jnp.where(position >= end, length, 0.0)
    return number, position - start


def attention_kernel(
    tok,
    routes,
    lengths,
    gains,
    router,
    frequency,
    wk_in,
    wv_in,
    wq_in,
    wo_in,
    g,
    h2_out,
    middle_out,
    mixed_out,
    h1_out,
    qpre_out,
    kpre_out,
    qa_out,
    kv_out,
    wq_out,
    wk_out,
    wv_out,
    wo_out,
    small_out,
    rope_out,
    aug_out,
    places_out,
    g_all,
    small,
    small_all,
    g_own,
    total,
    h2,
    middle,
    mixed,
    h1,
    qpre,
    kpre,
    qa,
    kv,
    wq,
    wk,
    wv,
    wo,
    params_low,
    rope,
    aug,
    places,
    local,
    leave,
    w_send,
    w_recv,
    k_send,
    k_recv,
    g_send,
    g_recv,
):
    me = Place()
    x, core = me.x, me.core
    right, left, sibling = me.along_x(1), me.along_x(-1), me.sibling()
    w_wires, k_wires, g_wires = Wires(w_send, w_recv), Wires(k_send, k_recv), Wires(g_send, g_recv)

    def shard(step):
        return (x + step + 4) % 4

    leaving = []

    def store(source, target):
        step = pltpu.make_async_copy(source, target, leave.at[len(leaving)])
        leaving.append(step)
        step.start()

    load_g = pltpu.make_async_copy(g, g_own.at[pl.ds(0, ROWS)], local.at[4])
    load_g.start()
    wide = lanes(1, 1024)
    row = lax.broadcasted_iota(jnp.int32, (16, 1024), 0)
    source = lax.broadcasted_iota(jnp.int32, (128, 1024), 0)
    here = wide // ROWS == x
    column = lanes(128, 1024)
    spread = ((column % 16 == source) & ((column % 64) // 16 == x)).astype(F32).astype(BF)

    def whole(gain):
        return jnp.where(here, jnp.concatenate([gain.astype(F32)] * 4, axis=1), 0.0)

    def tiled(gain):
        return dot(jnp.broadcast_to(gain, (16, 128)), spread)[0:1]

    block = jnp.zeros((16, 1024), F32)
    parts = (whole(gains[0:1, :]), whole(gains[1:2, :]), tiled(gains[2:3, 0:128]), tiled(gains[3:4, 0:128]))
    for n, part in enumerate(parts):
        block = jnp.where(row == n, part, block)
    small[pl.ds(0, 16), :] = block.astype(BF)
    small[pl.ds(16, 32), :] = whole(router[...]).astype(BF)

    expert = lax.broadcasted_iota(jnp.int32, (32, ROWS), 0)
    hits = sum(jnp.where(routes[k : k + 1, :] == expert, 1.0, 0.0) for k in range(8))
    before = (lax.broadcasted_iota(jnp.int32, (ROWS, ROWS), 0) < lanes(ROWS, ROWS)).astype(F32).astype(BF)
    places[...] = jnp.where(hits > 0.0, dot(hits.astype(BF), before), -1.0)
    packed = jnp.concatenate([places[q * 8 : (q + 1) * 8] for q in range(4)], axis=1)
    g_own[pl.ds(ROWS, 16), :] = jnp.concatenate([packed, jnp.zeros((8, 1024), F32)], axis=0).astype(BF)
    load_g.wait()
    greet([right, left, sibling, me.at(1, 0), me.at(-1, 0), me.at(0, 1), me.at(0, -1)])
    small_ring = GatherRing(w_wires, 0, lambda k, rows: small_all.at[shard(k), rows], small, right, left, 32, SMALL)
    small_ring.start()

    class Weight:
        def __init__(self, source, target, base):
            def at(k, rows, half):
                start = pl.multiple_of(shard(k) * ROWS + half * HALF + rows.start, 64)
                return target.at[pl.ds(start, rows.size), :]

            own = source.at[pl.ds(pl.multiple_of(core * HALF, HALF), HALF), :]
            full = pl.ds(0, HALF)
            self.ring = GatherRing(w_wires, base, lambda k, rows: at(k, rows, core), own, right, left, 64, HALF)
            self.pass_on = [
                w_wires.copy(at(k, full, core), at(k, full, core), base + 4 + n, sibling) for n, k in enumerate((-1, 1, 2))
            ]
            self.passed = [
                w_wires.copy(at(k, full, 1 - core), at(k, full, 1 - core), base + 4 + n, sibling)
                for n, k in enumerate((-1, 1, 2))
            ]
            self.keep = pltpu.make_async_copy(
                source, target.at[pl.ds(pl.multiple_of(x * ROWS, ROWS), ROWS), :], local.at[base // 7]
            )

        def start(self):
            self.ring.start()

        def forward(self):
            for way in range(2):
                self.ring.forward(way)
                self.pass_on[way].start()

        def finish(self):
            self.ring.wait_far()
            self.pass_on[2].start()

        def ready(self):
            for step in self.passed:
                step.wait_recv()

        def wait_sent(self):
            self.ring.wait_sent()
            for step in self.pass_on:
                step.wait_send()

    key_weight, value_weight = Weight(wk_in, wk, 4), Weight(wv_in, wv, 11)
    query_weight, out_weight = Weight(wq_in, wq, 18), Weight(wo_in, wo, 25)
    weights = [key_weight, value_weight, query_weight, out_weight]
    key_weight.start()
    value_weight.start()
    query_weight.keep.start()
    out_weight.keep.start()

    def g_at(fo):
        return lambda k, rows: g_all.at[me.block(fo, k), rows]

    first = GatherRing(
        g_wires, 0, lambda k, rows: g_all.at[me.block(k, 0), rows], g_own, me.at(1, 0), me.at(-1, 0), HALF, BLOCK
    )
    seconds = [
        GatherRing(
            g_wires,
            4 + 4 * i,
            g_at(fo),
            g_own if fo == 0 else g_all.at[me.block(fo, 0)],
            me.at(0, 1),
            me.at(0, -1),
            HALF,
            BLOCK,
        )
        for i, fo in enumerate((-1, 1, 2, 0))
    ]
    first.start()
    seconds[3].start()
    own_copies = [
        pltpu.make_async_copy(g_own, g_all.at[me.block(0, 0)], local.at[4]),
        pltpu.make_async_copy(small, small_all.at[x], local.at[5]),
        key_weight.keep,
        value_weight.keep,
    ]
    for step in own_copies:
        step.start()

    ends = lengths[...].astype(F32)
    doc, since = passed_documents(ends, ROWS, x * ROWS)
    lane = lanes()
    aug[pl.ds(0, ROWS), :] = jnp.where(
        lane.astype(F32) == doc, 16.0, jnp.where(lane == 8, -128.0, 0.0)
    ).astype(BF)
    angles = since * frequency[...]
    rope[0] = jnp.cos(angles)
    sine_table = jnp.sin(angles)
    rope[1] = jnp.where(lane % 64 < 32, -sine_table, sine_table)
    doc = passed_documents(ends, 1024, 0)[0]
    lane = lanes(1024)
    aug[pl.ds(ROWS, 1024), :] = jnp.where(
        lane.astype(F32) == doc, 8.0, jnp.where((lane >= 5) & (lane < 9), 1.0, 0.0)
    ).astype(BF)
    store(rope, rope_out)
    store(aug, aug_out)
    store(places, places_out)
    tokens = tok[...].astype(F32)
    tokens = tokens * lax.rsqrt(jnp.mean(tokens * tokens, axis=1, keepdims=True) + EPS)

    for way in range(2):
        small_ring.forward(way)
    key_weight.forward()
    value_weight.forward()
    query_weight.start()
    first.forward(0)
    seconds[0].start()
    first.forward(1)
    seconds[1].start()
    small_ring.wait_far()
    own_copies[1].wait()
    params = sum((small_all[k].astype(F32) for k in range(1, 4)), small_all[0].astype(F32))
    params_low[...] = params.astype(BF)
    store(params_low, small_out)
    h1[...] = (tokens * params[0:1]).astype(BF)
    store(h1, h1_out)
    key_weight.finish()
    value_weight.finish()
    key_weight.ready()
    key_weight.keep.wait()
    kpre[...] = dot(h1[...], wk[...])
    value_weight.ready()
    value_weight.keep.wait()
    kv[x, :, pl.ds(512, 512)] = dot(h1[...], wv[...]).astype(BF)
    keys = kpre[...]
    keys = keys * head_scale(keys, head_map(512)) * params[3:4, 0:512]
    for j in range(4):
        block = keys[:, j * 128 : (j + 1) * 128]
        kv[x, :, pl.ds(j * 128, 128)] = turn(block, rope[0], rope[1]).astype(BF)
    kv_ring = GatherRing(k_wires, 0, lambda k, rows: kv.at[shard(k), rows], kv.at[x], right, left, HALF, ROWS)
    query_weight.forward()
    kv_ring.start()
    store(kpre, kpre_out)
    store(wk, wk_out)
    store(wv, wv_out)
    first.wait_far()
    seconds[2].start()
    query_weight.finish()
    query_weight.ready()
    query_weight.keep.wait()
    qpre[...] = dot(h1[...], wq[...])
    store(qpre, qpre_out)
    store(wq, wq_out)
    queries = qpre[...]
    queries = queries * head_scale(queries, head_map(1024)) * params[2:3]
    for j in range(8):
        block = turn(queries[:, j * 128 : (j + 1) * 128], rope[0], rope[1]) * 0.125
        for n, head in enumerate(split_heads(block, j % 2 == 1)):
            start = ((j % 2) * 2 + n) * ROWS
            qa[j // 2, pl.ds(start, ROWS), pl.ds(0, 128)] = head.astype(BF)
            qa[j // 2, pl.ds(start, ROWS), pl.ds(128, 128)] = aug[pl.ds(0, ROWS), :]

    def attend(k):
        there = shard(k)
        marks = aug[pl.ds(pl.multiple_of(there * ROWS + ROWS, ROWS), ROWS), :]

        @pl.loop(0, HEAD_PAIRS)
        def _(pair):
            start = pl.multiple_of(pair * 128, 128)
            keyed = jnp.concatenate([kv[there, :, pl.ds(start, 128)], marks], axis=1)
            valued = jnp.concatenate([kv[there, :, pl.ds(start + 512, 128)], marks], axis=1)
            p = jnp.exp(dot(qa[pair], keyed, NT)).astype(BF)
            weighted = dot(p, valued)
            if k == 0:
                total[pair] = weighted
            else:
                total[pair] += weighted

    attend(0)
    kv_ring.forward(0)
    kv_ring.forward(1)
    out_weight.start()
    seconds[3].forward(0)
    seconds[3].forward(1)
    attend(-1)
    attend(1)
    for ring in seconds[0:2]:
        ring.forward(0)
        ring.forward(1)
    kv_ring.wait_far()
    attend(2)
    store(kv, kv_out)
    out_weight.forward()
    seconds[2].forward(0)
    seconds[2].forward(1)

    live = aug[pl.ds(0, ROWS), 4:5].astype(F32) == 0.0
    lane = lanes(1024)

    @pl.loop(0, HEAD_PAIRS)
    def _(pair):
        weighted = total[pair]
        mass = weighted[:, 133:134]
        heads = weighted[:, 0:128] / mass
        parts = three_parts(-jnp.log(mass))
        marks = qa[pair, :, pl.ds(128, 128)].astype(F32)
        for n, part in enumerate(parts):
            marks = jnp.where(lane == 5 + n, part, marks)
        qa[pair, :, pl.ds(128, 128)] = marks.astype(BF)
        heads = [heads[n * ROWS : (n + 1) * ROWS] for n in range(4)]
        for odd in range(2):
            joined = join_heads(heads[2 * odd], heads[2 * odd + 1], odd == 1)
            start = pl.multiple_of(pair * 256 + odd * 128, 128)
            mixed[:, pl.ds(start, 128)] = jnp.where(live, joined, 0.0).astype(BF)

    store(qa, qa_out)
    store(mixed, mixed_out)
    out_weight.finish()
    out_weight.ready()
    out_weight.keep.wait()
    store(wo, wo_out)
    middle[...] = tok[...].astype(F32) + dot(mixed[...], wo[...])
    store(middle, middle_out)
    scale = lax.rsqrt(jnp.mean(middle[...] * middle[...], axis=1, keepdims=True) + EPS)
    h2[...] = (middle[...] * scale * params_low[1:2, :].astype(F32)).astype(BF)
    store(h2, h2_out)
    for ring in [small_ring, kv_ring, first] + weights:
        ring.wait_sent()
    own_copies[0].wait()
    for ring in seconds:
        ring.wait_far()
    for ring in seconds:
        ring.wait_sent()
    for step in leaving:
        step.wait()


def attention_forward(*arrays):
    dma = pltpu.SemaphoreType.DMA
    s, v = jax.ShapeDtypeStruct, pltpu.VMEM
    stored = (
        ((ROWS, 1024), BF),
        ((ROWS, 1024), F32),
        ((ROWS, 1024), BF),
        ((ROWS, 1024), BF),
        ((ROWS, 1024), F32),
        ((ROWS, 512), F32),
        ((HEAD_PAIRS, 1024, 256), BF),
        ((4, ROWS, 1024), BF),
        ((1024, 1024), BF),
        ((1024, 512), BF),
        ((1024, 512), BF),
        ((1024, 1024), BF),
        ((SMALL, 1024), BF),
        ((2, ROWS, 128), F32),
        ((ROWS + 1024, 128), BF),
        ((32, ROWS), F32),
    )
    return call(
        attention_kernel,
        tuple(s(*one) for one in stored) + (s((16, BLOCK, 1024), BF),),
        [VMEM] * 6 + [ANY] * 5,
        (ANY,) * 17,
        [v((SMALL, 1024), BF), v((4, SMALL, 1024), BF), v((BLOCK, 1024), BF), v((HEAD_PAIRS, 1024, 256), F32)]
        + [v(*one) for one in stored]
        + [
            dma((6,)),
            dma((16,)),
            dma((32,)),
            dma((32,)),
            dma((4,)),
            dma((4,)),
            dma((20,)),
            dma((20,)),
        ],
        0,
        vmem=56,
    )(*arrays)


ORDER = (-1, 1, 2, 0)


def nth_place(i):
    return (3 + 2 * i + (i // 2) * 3) % 4


class ColumnWeight:
    def __init__(self, me, wires, base, source, target, by_rows, offset, half, rows, local):
        def at(k, part):
            start = pl.multiple_of(((me.x + k + 4) % 4) * 128 + offset, 128)
            if by_rows:
                return target.at[me.core, pl.ds(start, 128), :].at[part]
            return target.at[me.core, part, pl.ds(start, 128)]

        self.ring = GatherRing(wires, base, at, source, me.along_x(1), me.along_x(-1), half, rows)
        self.keep = pltpu.make_async_copy(source, at(0, pl.ds(0, rows)), local)
        mine, other = target.at[me.core], target.at[1 - me.core]
        if not by_rows:
            mine, other = mine.at[:, pl.ds(offset, 512)], other.at[:, pl.ds(offset, 512)]
        self.pass_on = wires.copy(mine, mine, base + 4, me.sibling())
        self.passed = wires.copy(other, other, base + 4, me.sibling())

    def start(self):
        self.ring.start()
        self.keep.start()

    def forward(self):
        self.ring.forward(0)
        self.ring.forward(1)

    def finish(self):
        self.ring.wait_far()
        self.keep.wait()
        self.pass_on.start()

    def wait_sent(self):
        self.ring.wait_sent()
        self.pass_on.wait_send()


def expert_kernel(
    h_ref,
    g_ref,
    router,
    gate_in,
    up_in,
    down_in,
    dx_out,
    y_out,
    own_g_out,
    own_u_out,
    own_d_out,
    pair_g_out,
    pair_u_out,
    pair_d_out,
    wgu,
    wd,
    wr,
    buf,
    gbuf,
    acc_gu,
    acc_d,
    near,
    landing,
    near_f,
    landing_f,
    xb,
    gxb,
    yb,
    dxb,
    act,
    dgu,
    hot,
    hot_t,
    weight,
    dgate,
    ystage,
    a_send,
    a_recv,
    r_send,
    r_recv,
    e_send,
    e_recv,
    p_send,
    p_recv,
    local,
    g_local,
    y_local,
):
    me = Place()
    f_right, f_left, s_right, s_left = me.at(1, 0), me.at(-1, 0), me.at(0, 1), me.at(0, -1)
    a_wires, r_wires = Wires(a_send, a_recv), Wires(r_send, r_recv)
    e_wires, p_wires = Wires(e_send, e_recv), Wires(p_send, p_recv)
    own = buf.at[me.block(0, 0), pl.ds(0, ROWS)]
    fetches = [
        pltpu.make_async_copy(h_ref, own, local.at[0]),
        pltpu.make_async_copy(router.at[pl.ds(ROUTER_ROW, 32), :], wr, local.at[1]),
    ]
    for step in fetches:
        step.start()
    gate_weight = ColumnWeight(me, e_wires, 0, gate_in, wgu, False, 0, 512, 1024, local.at[2])
    up_weight = ColumnWeight(me, e_wires, 5, up_in, wgu, False, 512, 512, 1024, local.at[3])
    down_weight = ColumnWeight(me, e_wires, 10, down_in, wd, True, 0, 64, 128, local.at[4])
    weights = [gate_weight, up_weight, down_weight]
    greet([f_right, f_left, s_right, s_left, me.along_x(1), me.along_x(-1), me.sibling()])
    order = nth_place

    first = GatherRing(
        a_wires, 0, lambda k, rows: buf.at[me.block(k, 0), rows], own, f_right, f_left, HALF, ROWS
    )

    def second(i):
        fo = order(i)

        def at(k, rows):
            return buf.at[me.block(fo, k), rows]

        return GatherRing(a_wires, 4 + 4 * i, at, at(0, pl.ds(0, ROWS)), s_right, s_left, HALF, ROWS)

    def reduce_second(i):
        fo = order(i)
        return ReduceRing(
            r_wires,
            4 + 4 * i,
            lambda k, rows: buf.at[me.block(fo, k), rows],
            lambda rows: near.at[i, rows],
            lambda way: landing.at[i, way],
            s_right,
            s_left,
            HALF,
            BLOCK,
        )

    reduce_first = ReduceRing(
        r_wires,
        0,
        lambda k, rows: buf.at[me.block(k, 0), rows],
        lambda rows: near_f.at[rows],
        lambda way: landing_f.at[way],
        f_right,
        f_left,
        HALF,
        BLOCK,
    )

    def load_g(i):
        start = ((me.first + order(i)) % 4) * 4
        return pltpu.make_async_copy(g_ref.at[pl.ds(start, 4)], gbuf.at[i % 2], g_local.at[i % 2])

    def store_y(i, j):
        return pltpu.make_async_copy(ystage.at[j], y_out.at[((me.first + order(i)) % 4) * 4 + j], y_local.at[j])

    fetches[0].wait()
    first.start()
    gate_weight.start()
    up_weight.start()
    load_g(0).start()
    for acc in (acc_gu, acc_d):

        @pl.loop(0, acc.shape[1] // 32)
        def _(r):
            acc[:, pl.ds(pl.multiple_of(r * 32, 32), 32), :] = jnp.zeros((2, 32, acc.shape[2]), F32)

    first.forward(0)
    second(0).start()
    first.forward(1)
    gate_weight.forward()
    up_weight.forward()
    down_weight.start()
    fetches[1].wait()
    gate_weight.finish()
    second(0).forward(0)
    second(0).forward(1)
    second(1).start()
    down_weight.forward()
    up_weight.finish()
    first.wait_far()
    second(2).start()

    expert_row = lax.broadcasted_iota(jnp.int32, (32, 256), 0)
    slot_row = lax.broadcasted_iota(jnp.int32, (CAP, 256), 0).astype(F32)
    low_row = lax.broadcasted_iota(jnp.int32, (8, 1024), 0)
    quarter = lax.broadcasted_iota(jnp.int32, (8, 1024), 1) // 256
    my_quarter = quarter == me.chip // 4
    my_low = 2 * (me.chip % 4)

    def pick(table, e):
        return jnp.sum(jnp.where(expert_row == 2 * me.chip + e, table, 0.0), axis=0, keepdims=True)

    @pl.loop(0, 4)
    def _(i):
        base = ((me.first + order(i)) % 4) * 4
        slot = i % 2
        second(i).wait_far()

        @pl.when(i < 3)
        def _():
            load_g(i + 1).start()

        load_g(i).wait()

        @pl.loop(0, 4)
        def _(j):
            h = buf[base + j, pl.ds(0, ROWS), :]
            g = gbuf[slot, j, pl.ds(0, ROWS), :]
            packed = gbuf[slot, j, pl.ds(ROWS, 16), :].astype(F32)[0:8]
            places = jnp.concatenate([packed[:, q * 256 : (q + 1) * 256] for q in range(4)], axis=0)
            logits = dot(wr[...], h, NT)
            routed = places >= 0.0
            top = jnp.max(jnp.where(routed, logits, -1e30), axis=0, keepdims=True)
            terms = jnp.where(routed, jnp.exp(jnp.where(routed, logits - top, 0.0)), 0.0)
            gates = terms / jnp.sum(terms, axis=0, keepdims=True)
            for e in range(2):
                hit = pick(places, e) == slot_row
                rows = pl.ds(e * CAP, CAP)
                weight[j, rows, :] = jnp.sum(jnp.where(hit, pick(gates, e), 0.0), axis=1, keepdims=True)
                hot[j, rows, :] = hit.astype(F32).astype(BF)
            hot_t[j] = jnp.transpose(hot[j].astype(F32)).astype(BF)
            xb[j] = dot(hot[j], h).astype(BF)
            gx = dot(hot[j], g)
            gxb[j] = gx.astype(BF)

        @pl.when(i > 0)
        def _():
            reduce_second(i - 1).middle(0)
            reduce_second(i - 1).middle(1)


        @pl.when(i == 0)
        def _():
            second(1).forward(0)
            second(1).forward(1)
            down_weight.finish()
            second(2).forward(0)
            second(2).forward(1)
            second(3).start()
            for step in weights:
                step.passed.wait_recv()

        @pl.when(i == 1)
        def _():
            second(3).forward(0)
            second(3).forward(1)

        @pl.loop(0, 2)
        def _(e):
            rows = pl.ds(pl.multiple_of(e * CAP, 32), CAP)
            x = xb[:, rows, :].reshape(4 * CAP, 1024)
            gx = gxb[:, rows, :].reshape(4 * CAP, 1024)
            gate = weight[:, rows, :].reshape(4 * CAP, 1)
            dy = (gate * gx.astype(F32)).astype(BF)
            both = dot(x, wgu[e])
            gate_pre, up_pre = both[:, 0:512], both[:, 512:1024]
            grad_act = dot(dy, wd[e], NT)
            sig = 1.0 / (1.0 + jnp.exp(-gate_pre))
            silu = gate_pre * sig
            active = (silu * up_pre).astype(BF)
            grad_gate = (grad_act * up_pre * (sig * (1.0 + gate_pre * (1.0 - sig)))).astype(BF)
            grad_up = (grad_act * silu).astype(BF)
            act[:, rows, :] = active.reshape(4, CAP, 512)
            dgu[:, rows, pl.ds(0, 512)] = grad_gate.reshape(4, CAP, 512)
            dgu[:, rows, pl.ds(512, 512)] = grad_up.reshape(4, CAP, 512)
            out = dot(active, wd[e]).astype(BF).astype(F32)
            dgate[:, rows, :] = jnp.sum(gx.astype(F32) * out, axis=1, keepdims=True).reshape(4, CAP, 1)
            yb[:, rows, :] = (gate * out).astype(BF).reshape(4, CAP, 1024)

        second(i).wait_sent()

        @pl.when(i == 0)
        def _():
            first.on[0].wait_send()

        @pl.when(i == 1)
        def _():
            first.on[1].wait_send()

        @pl.when(i == 3)
        def _():
            for step in first.go:
                step.wait_send()

        @pl.loop(0, 2)
        def _(e):
            rows = pl.ds(pl.multiple_of(e * CAP, 32), CAP)
            grad_in = dot(dgu[:, rows, :].reshape(4 * CAP, 1024), wgu[e], NT)
            dxb[:, rows, :] = grad_in.astype(BF).reshape(4, CAP, 1024)

        @pl.loop(0, 4)
        def _(j):
            buf[base + j, pl.ds(0, ROWS), :] = dot(hot_t[j], dxb[j]).astype(BF)
            spots = hot[j].astype(F32) * dgate[j]
            grad_rows = [jnp.sum(spots[e * CAP : (e + 1) * CAP], axis=0, keepdims=True) for e in range(2)]
            wide = [jnp.concatenate([row] * 4, axis=1) for row in grad_rows]
            mine = jnp.where(low_row == my_low, wide[0], jnp.where(low_row == my_low + 1, wide[1], 0.0))
            mine = jnp.where(my_quarter, mine, 0.0)
            high = mine.astype(BF).astype(F32)
            buf[base + j, pl.ds(ROWS, 16), :] = jnp.concatenate([high, mine - high], axis=0).astype(BF)

        reduce_second(i).start()

        @pl.when(i > 0)
        def _():
            reduce_second(i - 1).finish()

        @pl.when(i == 3)
        def _():
            reduce_first.start()

        @pl.loop(0, 4)
        def _(j):
            @pl.when(i > 0)
            def _():
                store_y(i - 1, j).wait()

            ystage[j] = dot(hot_t[j], yb[j]).astype(BF)
            store_y(i, j).start()


        @pl.when(i == 3)
        def _():
            reduce_second(3).middle(0)
            reduce_second(3).middle(1)

        @pl.loop(0, 2)
        def _(e):
            rows = pl.ds(pl.multiple_of(e * CAP, 32), CAP)
            x = xb[:, rows, :].reshape(4 * CAP, 1024)
            gate = weight[:, rows, :].reshape(4 * CAP, 1)
            dy = (gate * gxb[:, rows, :].reshape(4 * CAP, 1024).astype(F32)).astype(BF)
            grad_pre = dgu[:, rows, :].reshape(4 * CAP, 1024)
            active = act[:, rows, :].reshape(4 * CAP, 512)
            acc_gu[e] += dot(x, grad_pre, TN)
            acc_d[e] += dot(active, dy, TN)


    reduce_first.middle(0)
    reduce_first.middle(1)
    for j in range(4):
        store_y(3, j).wait()

    leaving = [None] * 4
    number = 0
    for acc, offset, width, own_out, pair_out in (
        (acc_d, 0, 1024, own_d_out, pair_d_out),
        (acc_gu, 0, 512, own_g_out, pair_g_out),
        (acc_gu, 512, 512, own_u_out, pair_u_out),
    ):
        for n in range(acc.shape[1] // 256):
            rows = pl.ds(n * 256, 256)
            for stays in (False, True):
                slot = (2 * number + stays) % 4
                if leaving[slot] is not None:
                    leaving[slot]()
                stage = ystage.at[slot, :, pl.ds(0, width)]
                stage[...] = acc[me.core if stays else 1 - me.core, rows, pl.ds(offset, width)].astype(BF)
                if stays:
                    step = pltpu.make_async_copy(stage, own_out.at[rows, :], y_local.at[slot])
                    leaving[slot] = step.wait
                else:
                    step = p_wires.copy(stage, pair_out.at[rows, :], number, me.sibling())
                    leaving[slot] = step.wait_send
                step.start()
            number += 1
    reduce_second(3).finish()
    mine = me.block(0, 0)
    for step in reduce_first.mid:
        step.wait_recv()
    add_into(buf.at[mine], landing_f.at[0], landing_f.at[1])
    result = pltpu.make_async_copy(buf.at[mine], dx_out, local.at[0])
    result.start()
    for step in leaving:
        step()
    number = 0
    for pair_out in (pair_d_out, pair_g_out, pair_u_out):
        for n in range(pair_out.shape[0] // 256):
            here = pair_out.at[pl.ds(n * 256, 256), :]
            p_wires.copy(here, here, number, me.sibling()).wait_recv()
            number += 1
    for step in range(4):
        reduce_second(step).wait_sent()
    reduce_first.wait_sent()
    for step in weights:
        step.wait_sent()
    result.wait()


def expert_stage(*arrays):
    dma = pltpu.SemaphoreType.DMA
    s, v = jax.ShapeDtypeStruct, pltpu.VMEM
    return call(
        expert_kernel,
        (
            s((BLOCK, 1024), BF),
            s((16, ROWS, 1024), BF),
            s((1024, 512), BF),
            s((1024, 512), BF),
            s((512, 1024), BF),
            s((1024, 512), BF),
            s((1024, 512), BF),
            s((512, 1024), BF),
        ),
        [ANY] * 6,
        (ANY,) * 8,
        [
            v((2, 1024, 1024), BF),
            v((2, 512, 1024), BF),
            v((32, 1024), BF),
            v((16, BLOCK, 1024), BF),
            v((2, 4, BLOCK, 1024), BF),
            v((2, 1024, 1024), F32),
            v((2, 512, 1024), F32),
            v((4, BLOCK, 1024), BF),
            v((4, 2, BLOCK, 1024), BF),
            v((BLOCK, 1024), BF),
            v((2, BLOCK, 1024), BF),
            v((4, 2 * CAP, 1024), BF),
            v((4, 2 * CAP, 1024), BF),
            v((4, 2 * CAP, 1024), BF),
            v((4, 2 * CAP, 1024), BF),
            v((4, 2 * CAP, 512), BF),
            v((4, 2 * CAP, 1024), BF),
            v((4, 2 * CAP, 256), BF),
            v((4, 256, 2 * CAP), BF),
            v((4, 2 * CAP, 1), F32),
            v((4, 2 * CAP, 1), F32),
            v((4, ROWS, 1024), BF),
            dma((20,)),
            dma((20,)),
            dma((20,)),
            dma((20,)),
            dma((15,)),
            dma((15,)),
            dma((10,)),
            dma((10,)),
            dma((5,)),
            dma((2,)),
            dma((4,)),
        ],
        1,
        vmem=62,
    )(*arrays)


Y_ORDER = (2, 1, -1, 0)


class Sum:
    def __init__(self, me, wires, base, own, pair, part_f, part_s, part_x, total):
        self.me, self.own, self.pair = me, own, pair
        self.parts = (part_f, part_s, part_x)
        sibling = me.sibling()

        def half_of(core):
            return pl.ds(pl.multiple_of(core * HALF, HALF), HALF)

        def cols_of(k):
            return pl.ds(pl.multiple_of(((me.first + k + 4) % 4) * 256, 256), 256)

        def rows_of(k):
            return pl.ds(pl.multiple_of(me.core * HALF + ((me.second + k + 4) % 4) * 32, 32), 32)

        def shard(k):
            return (me.x + k + 4) % 4

        kept = half_of(me.core)
        steps = (1, 2, 3)
        self.shards = [shard(k) for k in range(4)]
        self.kept, self.cols, self.rows = kept, cols_of(0), rows_of(0)
        self.swap = wires.copy(own.at[:, half_of(1 - me.core), :], pair, base, sibling)
        self.out_f = [wires.copy(own.at[:, kept, cols_of(k)], part_f.at[k - 1], base + k, me.at(k, 0)) for k in steps]
        self.out_s = [
            wires.copy(own.at[:, rows_of(k), cols_of(0)], part_s.at[k - 1], base + 3 + k, me.at(0, k)) for k in steps
        ]
        self.out_x = [
            wires.copy(own.at[shard(k), rows_of(0), cols_of(0)], part_x.at[k - 1], base + 6 + k, me.along_x(k))
            for k in steps
        ]

        def back(rows, cols, number, device):
            here = total.at[rows, cols]
            return wires.copy(here, here, number, device)

        self.result = total.at[rows_of(0), cols_of(0)]
        self.back_s = [back(rows_of(0), cols_of(0), base + 9 + k, me.at(0, k)) for k in steps]
        self.came_s = [back(rows_of(-k), cols_of(0), base + 9 + k, me.at(0, k)) for k in steps]
        self.back_f = [back(kept, cols_of(0), base + 12 + k, me.at(k, 0)) for k in steps]
        self.came_f = [back(kept, cols_of(-k), base + 12 + k, me.at(k, 0)) for k in steps]
        here, there = total.at[kept], total.at[half_of(1 - me.core)]
        self.last = wires.copy(here, here, base + 16, sibling)
        self.last_came = wires.copy(there, there, base + 16, sibling)

    def step(self, number):
        own, (part_f, part_s, part_x) = self.own, self.parts
        if number == 0:
            self.swap.start()
        elif number == 1:
            self.swap.wait_recv()
            for k in range(4):
                add_into(own.at[k, self.kept], self.pair.at[k])
            for copy in self.out_f:
                copy.start()
        elif number == 2:
            for copy in self.out_f:
                copy.wait_recv()
            for k in range(4):
                add_into(own.at[k, self.kept, self.cols], *[part_f.at[n, k] for n in range(3)])
            for copy in self.out_s:
                copy.start()
        elif number == 3:
            for copy in self.out_s:
                copy.wait_recv()
            for k in range(4):
                add_into(own.at[k, self.rows, self.cols], *[part_s.at[n, k] for n in range(3)])
            for copy in self.out_x:
                copy.start()
        elif number == 4:
            for copy in self.out_x:
                copy.wait_recv()
            add_up(self.result, own.at[self.me.x, self.rows, self.cols], *[part_x.at[n] for n in range(3)])
            for copy in self.back_s:
                copy.start()
        elif number == 5:
            for copy in self.came_s:
                copy.wait_recv()
            for copy in self.back_f:
                copy.start()
        elif number == 6:
            for copy in self.came_f:
                copy.wait_recv()
            self.last.start()
        else:
            self.last_came.wait_recv()

    def wait_sent(self):
        for copy in [self.swap, self.last] + self.out_f + self.out_s + self.out_x + self.back_s + self.back_f:
            copy.wait_send()


LOADED = {
    "summed": ((BLOCK, 1024), BF),
    "h2": ((ROWS, 1024), BF),
    "middle": ((ROWS, 1024), F32),
    "cot": ((ROWS, 1024), BF),
    "tok": ((ROWS, 1024), BF),
    "mixed": ((ROWS, 1024), BF),
    "h1": ((ROWS, 1024), BF),
    "qpre": ((ROWS, 1024), F32),
    "kpre": ((ROWS, 512), F32),
    "qa": ((HEAD_PAIRS, 1024, 256), BF),
    "kv": ((4, ROWS, 1024), BF),
    "wk": ((1024, 512), BF),
    "wv": ((1024, 512), BF),
    "small": ((SMALL, 1024), BF),
    "rope": ((2, ROWS, 128), F32),
    "aug": ((ROWS + 1024, 128), BF),
    "places": ((32, ROWS), F32),
}


def backward_kernel(*refs):
    sources, refs = dict(zip(LOADED, refs)), refs[len(LOADED) :]
    wq, wo, gw, uw, dw, gp, up, dp, y, layer_out, tokens_out, total_out, small_out, g_out, u_out, d_out = refs[:16]
    refs = refs[16:]
    held, refs = dict(zip(LOADED, refs)), refs[len(LOADED) :]
    (
        doa,
        dqa,
        dkv,
        wbuf,
        parts,
        pair_w,
        part_f,
        part_s,
        part_x,
        total_w,
        near_k,
        land_k,
        own_g,
        own_u,
        own_d,
        pair_g,
        pair_u,
        pair_d,
        near_g,
        near_u,
        near_d,
        land_g,
        land_u,
        land_d,
        buf,
        y_sum,
        near_s,
        land_s,
        near_f,
        land_f,
        small_part,
        small_pair,
        small_x,
        small_f,
        small_s,
        layer,
        grad_middle,
        small_total,
        final_g,
        final_u,
        final_d,
        e_send,
        e_recv,
        w_send,
        w_recv,
        k_send,
        k_recv,
        y_send,
        y_recv,
        t_send,
        t_recv,
        local,
        fetched,
        leave,
    ) = refs
    summed, h2, middle, cot, tok, mixed, h1, qpre, kpre, qa, kv, wk, wv, small, rope, aug, places = held.values()
    me = Place()
    x, core = me.x, me.core
    right, left, sibling = me.along_x(1), me.along_x(-1), me.sibling()
    planes = [me.at(1, 0), me.at(-1, 0), me.at(2, 0), me.at(0, 1), me.at(0, -1), me.at(0, 2)]
    e_wires, w_wires, k_wires = Wires(e_send, e_recv), Wires(w_send, w_recv), Wires(k_send, k_recv)
    y_wires, t_wires = Wires(y_send, y_recv), Wires(t_send, t_recv)

    def shard(step):
        return (x + step + 4) % 4

    loads = {
        name: pltpu.make_async_copy(sources[name], held[name], fetched.at[n]) for n, name in enumerate(LOADED)
    }
    pulls = [
        pltpu.make_async_copy(source, target, local.at[n])
        for n, (source, target) in enumerate(
            ((gw, own_g), (uw, own_u), (dw, own_d), (gp, pair_g), (up, pair_u), (dp, pair_d), (wo, wbuf))
        )
    ]
    load_wq = pltpu.make_async_copy(wq, wbuf, local.at[7])

    def load_y(i):
        start = ((me.first + Y_ORDER[i] + 4) % 4) * 4
        return pltpu.make_async_copy(y.at[pl.ds(start, 4)], buf.at[i % 2], local.at[8 + i % 2])

    def ready(*names):
        for name in names:
            loads[name].wait()

    leaving = []

    def store(source, target):
        step = pltpu.make_async_copy(source, target, leave.at[len(leaving)])
        leaving.append(step)
        step.start()

    for step in pulls[:6]:
        step.start()
    load_y(0).start()
    for name in ("summed", "h2", "small", "places", "middle", "cot", "mixed"):
        loads[name].start()
    pulls[6].start()
    load_y(1).start()
    for name in ("aug", "qa", "kv", "rope", "qpre", "kpre", "h1", "wk", "wv", "tok"):
        loads[name].start()
    greet([right, left, me.along_x(2), sibling] + planes)

    def y_second(i):
        return ReduceRing(
            y_wires,
            4 + 4 * i,
            lambda k, rows: buf.at[i % 2, (me.second + k + 4) % 4, rows],
            lambda rows: near_s.at[i % 2, rows],
            lambda way: land_s.at[i % 2, way],
            me.at(0, 1),
            me.at(0, -1),
            HALF,
            ROWS,
        )

    y_first = ReduceRing(
        y_wires,
        0,
        lambda k, rows: y_sum.at[(me.first + k + 4) % 4, rows],
        lambda rows: near_f.at[rows],
        lambda way: land_f.at[way],
        me.at(1, 0),
        me.at(-1, 0),
        HALF,
        ROWS,
    )
    y_rings = [y_second(i) for i in range(4)]

    def y_start(i):
        load_y(i).wait()
        y_rings[i].start()

    def y_finish(i):
        y_rings[i].finish(y_sum.at[(me.first + Y_ORDER[i] + 4) % 4])
        y_rings[i].wait_sent()
        if i < 2:
            load_y(i + 2).start()

    def weight_sum(n, own):
        return Sum(
            me,
            w_wires,
            17 * n,
            own,
            pair_w.at[n % 2],
            part_f.at[n],
            part_s.at[n],
            part_x.at[n],
            total_w.at[n],
        )

    out_sum, query_sum, kv_sum = weight_sum(0, parts.at[0]), weight_sum(1, parts.at[1]), weight_sum(2, dkv)

    def weight_grad(target, left_rows, right_rows):
        for k in range(4):
            target[k] = dot(left_rows[:, k * ROWS : (k + 1) * ROWS], right_rows, TN).astype(BF)

    def slice_of(k):
        return pl.ds(pl.multiple_of(shard(k) * 128, 128), 128)

    def g_at(k, ref=None):
        return (own_g if ref is None else ref).at[:, slice_of(k)]

    def u_at(k, ref=None):
        return (own_u if ref is None else ref).at[:, slice_of(k)]

    def d_at(k, start=0, size=128, ref=None):
        return (own_d if ref is None else ref).at[pl.ds(pl.multiple_of(shard(k) * 128 + start, 64), size), :]

    e_far = [
        e_wires.copy(g_at(2), near_g, 3, right),
        e_wires.copy(d_at(2, 0, 64), near_d.at[0], 4, right),
        e_wires.copy(u_at(2), near_u, 5, left),
        e_wires.copy(d_at(2, 64, 64), near_d.at[1], 6, left),
    ]
    e_mid = [
        e_wires.copy(ref, land.at[way], 7 + way * 3 + i, device)
        for way, (k, device) in enumerate(((1, right), (-1, left)))
        for i, (ref, land) in enumerate(((g_at(k), land_g), (u_at(k), land_u), (d_at(k), land_d)))
    ]

    def add_pair(k):
        add_into(g_at(k), g_at(k, pair_g))
        add_into(u_at(k), u_at(k, pair_u))
        add_into(d_at(k), d_at(k, ref=pair_d))

    for step in pulls[:6]:
        step.wait()
    add_pair(2)
    for step in e_far:
        step.start()
    y_start(0)
    y_start(1)

    ready("summed", "h2", "small", "places")
    params = small[...].astype(F32)
    h2_rows = h2[...]
    numbers = summed[pl.ds(ROWS, 16), :].astype(F32)
    numbers = numbers[0:8] + numbers[8:16]
    grad_gates = jnp.concatenate([numbers[:, q * 256 : (q + 1) * 256] for q in range(4)], axis=0)
    logits = dot(small[pl.ds(ROUTER_ROW, 32), :], h2_rows, NT)
    routed = places[...] >= 0.0
    top = jnp.max(jnp.where(routed, logits, -1e30), axis=0, keepdims=True)
    terms = jnp.where(routed, jnp.exp(jnp.where(routed, logits - top, 0.0)), 0.0)
    gates = terms / jnp.sum(terms, axis=0, keepdims=True)
    grad_logits = gates * (grad_gates - jnp.sum(gates * grad_gates, axis=0, keepdims=True))
    grad_router = split_dot(grad_logits, h2_rows)
    for k in range(4):
        small_part[k, pl.ds(0, 32), :] = grad_router[:, k * ROWS : (k + 1) * ROWS]
        small_part[k, pl.ds(32, 16), :] = jnp.zeros((16, ROWS), F32)
    grad = summed[pl.ds(0, ROWS), :].astype(F32) + split_dot(grad_logits, small[pl.ds(ROUTER_ROW, 32), :], TN)

    def norm_back(v, gain, grad, row):
        scale = lax.rsqrt(jnp.mean(v * v, axis=1, keepdims=True) + EPS)
        normed = v * scale
        gained = gain * grad
        gain_grad = jnp.sum(grad * normed, axis=0, keepdims=True)
        for k in range(4):
            small_part[k, row : row + 1, :] = gain_grad[:, k * ROWS : (k + 1) * ROWS]
        return scale * (gained - normed * jnp.mean(gained * normed, axis=1, keepdims=True))

    ready("middle", "cot", "mixed")
    grad_middle[...] = cot[...].astype(F32) + norm_back(middle[...], params[1:2], grad, 33)
    grad_low = grad_middle[...].astype(BF)
    grad_low = grad_middle[...].astype(BF)
    ready("aug")
    live = aug[pl.ds(0, ROWS), 4:5].astype(F32) == 0.0
    pulls[6].wait()
    grad_mixed = jnp.where(live, dot(grad_low, wbuf[...], NT), 0.0).astype(BF).astype(F32)
    row_dots = split_dot(grad_mixed * mixed[...].astype(F32), head_map(1024))
    lane = lanes()
    for j in range(8):
        for n, head in enumerate(split_heads(grad_mixed[:, j * 128 : (j + 1) * 128], j % 2 == 1)):
            start = ((j % 2) * 2 + n) * ROWS
            marks = jnp.zeros((ROWS, 128), F32)
            for m, part in enumerate(three_parts(-row_dots[:, 2 * j + n : 2 * j + n + 1])):
                marks = jnp.where(lane == 5 + m, part, marks)
            doa[j // 2, pl.ds(start, ROWS), pl.ds(0, 128)] = head.astype(BF)
            doa[j // 2, pl.ds(start, ROWS), pl.ds(128, 128)] = marks.astype(BF)

    load_wq.start()
    ready("qa", "kv")

    def attend(k):
        there = shard(k)
        marks = aug[pl.ds(pl.multiple_of(there * ROWS + ROWS, ROWS), ROWS), :]

        @pl.loop(0, HEAD_PAIRS)
        def _(pair):
            start = pl.multiple_of(pair * 128, 128)
            keys = kv[there, :, pl.ds(start, 128)]
            keyed = jnp.concatenate([keys, marks], axis=1)
            valued = jnp.concatenate([kv[there, :, pl.ds(start + 512, 128)], marks], axis=1)
            p = jnp.exp(dot(qa[pair], keyed, NT))
            ds = (p * dot(doa[pair], valued, NT)).astype(BF)
            dkv[there, :, pl.ds(start + 512, 128)] = dot(p.astype(BF), doa[pair, :, pl.ds(0, 128)], TN).astype(BF)
            dkv[there, :, pl.ds(start, 128)] = dot(ds, qa[pair, :, pl.ds(0, 128)], TN).astype(BF)
            dq = dot(ds, keys)
            if k == 2:
                dqa[pair] = dq
            else:
                dqa[pair] += dq

    kv_ring = ReduceRing(
        k_wires,
        0,
        lambda k, rows: dkv.at[shard(k), rows],
        lambda rows: near_k.at[rows],
        lambda way: land_k.at[way],
        right,
        left,
        HALF,
        ROWS,
    )
    attend(2)
    kv_ring.start()
    y_rings[0].middle_both()
    y_rings[1].middle_both()
    weight_grad(parts.at[0], mixed[...], grad_low)
    out_sum.step(0)
    for k in (1, -1, 0):
        add_pair(k)
    attend(1)
    kv_ring.middle(0)
    out_sum.step(1)
    y_finish(0)
    y_finish(1)
    attend(-1)
    kv_ring.middle(1)
    y_first.start()
    y_start(2)
    y_start(3)
    e_far[0].wait_recv()
    add_into(g_at(1), near_g)
    e_far[1].wait_recv()
    add_into(d_at(1, 0, 64), near_d.at[0])
    e_far[2].wait_recv()
    add_into(u_at(-1), near_u)
    e_far[3].wait_recv()
    add_into(d_at(-1, 64, 64), near_d.at[1])
    for step in e_mid:
        step.start()
    attend(0)
    out_sum.step(2)
    y_rings[2].middle_both()
    y_rings[3].middle_both()

    def heads_back(pre, grads, gain, count):
        heads = head_map(count)
        scale = head_scale(pre, heads)
        normed = pre * scale
        gained = gain * grads
        mean = split_dot(split_dot(gained * normed, heads) * (1.0 / 64), heads, NT)
        gain_grad = jnp.sum(grads * normed, axis=0, keepdims=True)
        folded = sum(gain_grad[:, j * 128 : (j + 1) * 128] for j in range(count // 128))
        return scale * (gained - normed * mean), folded

    ready("rope", "qpre", "h1")
    blocks = []
    for j in range(8):
        pair, odd = j // 2, j % 2 == 1
        heads = [dqa[pair, pl.ds(((j % 2) * 2 + n) * ROWS, ROWS), :] for n in range(2)]
        blocks.append(turn(join_heads(heads[0], heads[1], odd) * 0.125, rope[0], -rope[1]))
    query_grad, query_gain_grad = heads_back(qpre[...], jnp.concatenate(blocks, axis=1), params[2:3], 1024)
    query_low = query_grad.astype(BF)
    weight_grad(parts.at[1], h1[...], query_low)
    query_sum.step(0)
    load_wq.wait()
    grad_h1 = dot(query_low, wbuf[...], NT)

    ready("kpre")
    kv_ring.finish()
    own_kv = dkv[x].astype(F32)
    blocks = [turn(own_kv[:, j * 128 : (j + 1) * 128], rope[0], -rope[1]) for j in range(4)]
    key_grad, key_gain_grad = heads_back(kpre[...], jnp.concatenate(blocks, axis=1), params[3:4, 0:512], 512)
    low = jnp.concatenate([key_grad.astype(BF), own_kv[:, 512:1024].astype(BF)], axis=1)
    kv_ring.wait_sent()
    weight_grad(dkv, h1[...], low)
    query_sum.step(1)
    kv_sum.step(0)
    ready("wk", "wv", "tok")
    grad_h1 = grad_h1 + dot(low[:, 0:512], wk[...], NT) + dot(low[:, 512:1024], wv[...], NT)
    grad_middle[...] += norm_back(tok[...].astype(F32), params[0:1], grad_h1, 32)
    store(grad_middle, tokens_out)
    for k in range(4):
        small_part[k, 34:35, pl.ds(0, 128)] = query_gain_grad
        small_part[k, 35:36, pl.ds(0, 128)] = key_gain_grad

    t_pair = t_wires.copy(small_part, small_pair, 0, sibling)
    t_pair.start()
    kv_sum.step(1)
    out_sum.step(3)
    y_finish(2)
    y_finish(3)
    y_first.middle_both()
    query_sum.step(2)
    t_pair.wait_recv()
    t_x = [t_wires.copy(small_part.at[shard(k)], small_x.at[k - 1], k, me.along_x(k)) for k in (1, 2, 3)]
    t_pair.wait_send()
    for k in range(4):
        small_part[k] += small_pair[k]
    for step in t_x:
        step.start()
    kv_sum.step(2)
    query_sum.step(3)
    kv_sum.step(3)
    out_sum.step(4)
    for step in t_x:
        step.wait_recv()
    small_f[0] = small_part[x] + small_x[0] + small_x[1] + small_x[2]
    t_f = [t_wires.copy(small_f.at[0], small_f.at[k], 3 + k, me.at(k, 0)) for k in (1, 2, 3)]
    for step in t_f:
        step.start()
    query_sum.step(4)
    kv_sum.step(4)
    out_sum.step(5)
    for step in t_f:
        step.wait_recv()
    small_s[0] = small_f[0] + small_f[1] + small_f[2] + small_f[3]
    t_s = [t_wires.copy(small_s.at[0], small_s.at[k], 6 + k, me.at(0, k)) for k in (1, 2, 3)]
    for step in t_s:
        step.start()
    query_sum.step(5)
    kv_sum.step(5)
    out_sum.step(6)
    for step in e_mid:
        step.wait_recv()
    for out, at, land, target in (
        (final_g, g_at, land_g, g_out),
        (final_u, u_at, land_u, u_out),
        (final_d, d_at, land_d, d_out),
    ):
        add_up(out, at(0), land.at[0], land.at[1])
        store(out, target)
    query_sum.step(6)
    kv_sum.step(6)
    for step in t_s:
        step.wait_recv()
    small_total[...] = small_s[0] + small_s[1] + small_s[2] + small_s[3]
    store(small_total, small_out)
    out_sum.step(7)
    store(total_w.at[0], total_out.at[0])
    y_first.finish()
    layer[...] = (middle[...] + y_sum[me.first].astype(F32)).astype(BF)
    store(layer, layer_out)
    query_sum.step(7)
    store(total_w.at[1], total_out.at[1])
    kv_sum.step(7)
    store(total_w.at[2], total_out.at[2])
    for step in e_far + e_mid + t_x + t_f + t_s:
        step.wait_send()
    for ring in [y_first, out_sum, query_sum, kv_sum]:
        ring.wait_sent()
    for step in leaving:
        step.wait()


def backward_stage(*arrays):
    dma = pltpu.SemaphoreType.DMA
    s, v = jax.ShapeDtypeStruct, pltpu.VMEM
    return call(
        backward_kernel,
        (
            s((ROWS, 1024), BF),
            s((ROWS, 1024), F32),
            s((3, ROWS, 1024), BF),
            s((SMALL, ROWS), F32),
            s((1024, 128), F32),
            s((1024, 128), F32),
            s((128, 1024), F32),
        ),
        [ANY] * (len(LOADED) + 9),
        (ANY,) * 7,
        [v(*one) for one in LOADED.values()]
        + [
            v((HEAD_PAIRS, 1024, 256), BF),
            v((HEAD_PAIRS, 1024, 128), F32),
            v((4, ROWS, 1024), BF),
            v((1024, 1024), BF),
            v((2, 4, ROWS, 1024), BF),
            v((2, 4, HALF, 1024), BF),
            v((3, 3, 4, HALF, 256), BF),
            v((3, 3, 4, 32, 256), BF),
            v((3, 3, 32, 256), BF),
            v((3, ROWS, 1024), BF),
            v((ROWS, 1024), BF),
            v((2, ROWS, 1024), BF),
            v((1024, 512), BF),
            v((1024, 512), BF),
            v((512, 1024), BF),
            v((1024, 512), BF),
            v((1024, 512), BF),
            v((512, 1024), BF),
            v((1024, 128), BF),
            v((1024, 128), BF),
            v((2, 64, 1024), BF),
            v((2, 1024, 128), BF),
            v((2, 1024, 128), BF),
            v((2, 128, 1024), BF),
            v((2, 4, ROWS, 1024), BF),
            v((4, ROWS, 1024), BF),
            v((2, ROWS, 1024), BF),
            v((2, 2, ROWS, 1024), BF),
            v((ROWS, 1024), BF),
            v((2, ROWS, 1024), BF),
            v((4, SMALL, ROWS), F32),
            v((4, SMALL, ROWS), F32),
            v((3, SMALL, ROWS), F32),
            v((4, SMALL, ROWS), F32),
            v((4, SMALL, ROWS), F32),
            v((ROWS, 1024), BF),
            v((ROWS, 1024), F32),
            v((SMALL, ROWS), F32),
            v((1024, 128), F32),
            v((1024, 128), F32),
            v((128, 1024), F32),
            dma((13,)),
            dma((13,)),
            dma((51,)),
            dma((51,)),
            dma((4,)),
            dma((4,)),
            dma((20,)),
            dma((20,)),
            dma((10,)),
            dma((10,)),
            dma((10,)),
            dma((len(LOADED),)),
            dma((9,)),
        ],
        2,
        vmem=63,
    )(*arrays)


def last_kernel(layer, tokens, totals, small, g, u, d, *rest):
    outs, (layer_v, tokens_v, totals_v, small_v, g_v, u_v, d_v), held, sem = rest[:13], rest[13:20], rest[20:24], rest[24]
    sources = (totals, small, tokens, layer, g, u, d)
    inside = (totals_v, small_v, tokens_v, layer_v, g_v, u_v, d_v)
    loads = [pltpu.make_async_copy(source, inner, sem.at[n]) for n, (source, inner) in enumerate(zip(sources, inside))]
    for step in loads:
        step.start()
    layer_out, tokens_out, g_out, u_out, d_out, wq, wk, wv, wo, first, second, heads, router = outs
    wq_v, wk_v, wv_v, wo_v = held
    stores = []

    def store(source, target):
        step = pltpu.make_async_copy(source, target, sem.at[7 + len(stores)])
        stores.append(step)
        step.start()

    loads[0].wait()
    wq_v[...] = totals_v[1].astype(F32)
    store(wq_v, wq)
    wo_v[...] = totals_v[0].astype(F32)
    store(wo_v, wo)
    wk_v[...] = totals_v[2, :, pl.ds(0, 512)].astype(F32)
    store(wk_v, wk)
    wv_v[...] = totals_v[2, :, pl.ds(512, 512)].astype(F32)
    store(wv_v, wv)
    loads[1].wait()
    first[...] = small_v[32:33, :]
    second[...] = small_v[33:34, :]
    both = small_v[34:36, 0:128]
    heads[...] = both + pltpu.roll(both, 64, 1)
    router[...] = small_v[0:32, :]
    for step, inner, target in zip(loads[2:], inside[2:], (tokens_out, layer_out, g_out, u_out, d_out)):
        step.wait()
        store(inner, target)
    for step in stores:
        step.wait()


def last_stage(*arrays):
    s, v = jax.ShapeDtypeStruct, pltpu.VMEM
    return pl.pallas_call(
        last_kernel,
        out_shape=(
            s((ROWS, 1024), BF),
            s((ROWS, 1024), F32),
            s((1024, 128), F32),
            s((1024, 128), F32),
            s((128, 1024), F32),
            s((ROWS, 1024), F32),
            s((ROWS, 512), F32),
            s((ROWS, 512), F32),
            s((ROWS, 1024), F32),
            s((1, ROWS), F32),
            s((1, ROWS), F32),
            s((2, 128), F32),
            s((32, ROWS), F32),
        ),
        in_specs=[ANY] * 7,
        out_specs=(ANY,) * 9 + (VMEM,) * 4,
        scratch_shapes=[
            v((ROWS, 1024), BF),
            v((ROWS, 1024), F32),
            v((3, ROWS, 1024), BF),
            v((SMALL, ROWS), F32),
            v((1024, 128), F32),
            v((1024, 128), F32),
            v((128, 1024), F32),
            v((ROWS, 1024), F32),
            v((ROWS, 512), F32),
            v((ROWS, 512), F32),
            v((ROWS, 1024), F32),
            pltpu.SemaphoreType.DMA((16,)),
        ],
        compiler_params=pltpu.CompilerParams(vmem_limit_bytes=62 * MIB),
    )(*arrays)


def body(
    tokens,
    lengths,
    routes,
    norm1_gain,
    w_query,
    w_key,
    w_value,
    query_gain,
    key_gain,
    w_out,
    norm2_gain,
    w_router,
    w_gate,
    w_up,
    w_down,
    cotangent,
):
    x = lax.axis_index("shard")
    frequency = (ROPE_BASE ** -((np.arange(128) % 32) / 32.0)).astype(np.float32)[None]
    gains = jnp.concatenate(
        [norm1_gain, norm2_gain, jnp.pad(query_gain, (0, ROWS - 16)), jnp.pad(key_gain, (0, ROWS - 16))]
    ).reshape(4, ROWS)
    (h2, middle, mixed, h1, qpre, kpre, qa, kv, wq, wk, wv, wo, small, rope, aug, places, g_all) = attention_forward(
        tokens,
        routes.T,
        lengths,
        gains,
        w_router.T,
        jnp.asarray(frequency),
        w_key,
        w_value,
        w_query,
        w_out,
        cotangent,
    )
    summed, y_part, *expert_grads = expert_stage(
        h2, g_all, small, w_gate[0], w_up[0], w_down[0]
    )
    results = backward_stage(
        summed,
        h2,
        middle,
        cotangent,
        tokens,
        mixed,
        h1,
        qpre,
        kpre,
        qa,
        kv,
        wk,
        wv,
        small,
        rope,
        aug,
        places,
        wq,
        wo,
        *expert_grads,
        y_part,
    )
    layer, tokens_grad, gate_grad, up_grad, down_grad, wq_g, wk_g, wv_g, wo_g, first, second, heads, router = last_stage(
        *results
    )
    heads = lax.dynamic_slice(heads, (0, x * 16), (2, 16))
    return (
        layer,
        tokens_grad,
        first[0],
        wq_g,
        wk_g,
        wv_g,
        heads[0],
        heads[1],
        wo_g,
        second[0],
        router.T,
        gate_grad[None],
        up_grad[None],
        down_grad[None],
    )


def solution(mesh):
    rows = P(("expert", "shard"), None)
    by_shard = P("shard", None)
    columns = P("expert", None, "shard")
    placed = (
        rows,
        P("expert", None),
        rows,
        P("shard"),
        by_shard,
        by_shard,
        by_shard,
        P("shard"),
        P("shard"),
        by_shard,
        P("shard"),
        by_shard,
        columns,
        columns,
        P("expert", "shard", None),
        rows,
    )
    return jax.shard_map(
        body,
        mesh=mesh,
        in_specs=placed,
        out_specs=(
            rows,
            rows,
            P("shard"),
            by_shard,
            by_shard,
            by_shard,
            P("shard"),
            P("shard"),
            by_shard,
            P("shard"),
            by_shard,
            columns,
            columns,
            P("expert", "shard", None),
        ),
        check_vma=False,
    )
```

time: 563 us -> 291 us (0.52)
  matrix products: 120 us -> 0 us
  local copies, waits for them, and re-layouts: 67 us -> 1.85 us
  other arithmetic: 34.2 us -> 0.72 us
  waiting for transfers between devices: 23.2 us -> 0 us
  between operations: 14.6 us -> 0.68 us
  Pallas kernels: 297 us -> 286 us
    dot_general x22 -> x0, matrix products: 120 us -> none  [the longest x1 24.4 us: body(): jnp.einsum('kgts,tkgd->skd', grad_scores, query_grouped, preferred_elemen...]
    unnamed x89 -> x0, local copies, waits for them, and re-layouts: 22.7 us -> none
    concatenate x3 -> x0, local copies, waits for them, and re-layouts: 14.6 us -> none  [the longest x1 12 us: body(): jnp.concatenate([grad_query_w.astype(BF), grad_key_w.astype(BF), grad_val...]
    all_gather x2 -> x0, waiting for transfers between devices: 13.6 us -> none  [the longest x1 9.33 us: body(): lax.all_gather(value_low, 'shard', axis=0, tiled=True)]
    reduce_sum x9 -> x0, other arithmetic: 13 us -> none  [the longest x1 8.25 us: body(): denominator = jnp.sum(exponent_terms, axis=-1, keepdims=True)]
    slice x7 -> x0, local copies, waits for them, and re-layouts: 12.5 us -> none  [the longest x1 4.16 us: body(): out_full = wall_full[:, :, 2048:3072].reshape(1024, 1024)]
    pallas_call x3 -> x4, Pallas kernels: 297 us -> 286 us  [the longest x1 119 us: expert_stage(): call(expert_kernel, (s((BLOCK, 1024), BF), s((16, ROWS, 1024), BF), s((10...]
    reduce_scatter x2 -> x0, waiting for transfers between devices: 9.55 us -> none  [the longest x1 9.55 us: body(): lax.psum_scatter(grad_values.reshape(length, kv_heads * head_dim).astype(...]
  transfers between devices with their start and end apart: 4 -> 0, of which waited for: 3 -> 0; matrix products, arithmetic and copies ran while one was open for 13% -> 0% of each run, Pallas kernels for 0% -> 0%
where the time goes in v2:
time: 291 us; the launch traced here: 289 us
  Pallas kernels  286 us (98%)
    pallas_call x1, Pallas kernels, expert_stage(): call(expert_kernel, (s((BLOCK, 1024), BF), s((16, ROWS, 1024), BF), s((10...  119 us
    pallas_call x1, Pallas kernels, backward_stage(): call(backward_kernel, (s((ROWS, 1024), BF), s((ROWS, 1024), F32), s((3, R...  99.6 us
    pallas_call x1, Pallas kernels, attention_forward(): call(attention_kernel, tuple((s(*one) for one in stored)) + (s((16, BLOCK...  62.5 us

profile of v2, /device:TPU:0, one launch (start us, length us, event | category | flops | bytes accessed | tf_op | source)
XLA Modules:
  0.0 289.2 jit_solution(3642351553535283503)
XLA Ops:
  0.6 0.7 fusion.4
  1.4 0.6 reshape.31.gains
  1.9 62.5 %shard_map.272 = (bf16[256,1024]{1,0:T(8,128)(2,1)}, f32[256,1024]{1,0:T(8,128)}, bf16[256,1024]{1,0:T(8,128)(2,1)}, bf16[256,1024]{1,0:T(8,128)(2,1)}, f32[256,...) custom-call(bf16[256,1024]{1,0:T(8,128)(2,1)} %refs_4_.1, ...), custom_call_target="tpu_custom_call" | custom-call | tf_op jit(solution)/shard_map/pallas_call | solution.py:607
  64.5 118.9 %shard_map.273 = (bf16[272,1024]{1,0:T(8,128)(2,1)}, bf16[16,256,1024]{2,1,0:T(8,128)(2,1)}, bf16[1024,512]{1,0:T(8,128)(2,1)}, bf16[1024,512]{1,0:T(8,128)(2,1)...) custom-call(bf16[256,1024]{1,0:T(8,128)(2,1)} %get-tuple-element.59., ...), custom_call_target="tpu_custom_call" | custom-call | tf_op jit(solution)/shard_map/pallas_call | solution.py:1019
  183.4 99.6 %shard_map.274 = (bf16[256,1024]{1,0:T(8,128)(2,1)}, f32[256,1024]{1,0:T(8,128)}, bf16[3,256,1024]{2,1,0:T(8,128)(2,1)}, f32[48,256]{1,0:T(8,128)}, f32[1024,128...) custom-call(bf16[272,1024]{1,0:T(8,128)(2,1)} %get-tuple-element.62.refs_0_, ...), custom_call_target="tpu_custom_call" | custom-call | tf_op jit(solution)/shard_map/pallas_call | solution.py:1616
  283.0 4.9 %shard_map.275 = (bf16[256,1024]{1,0:T(8,128)(2,1)}, f32[256,1024]{1,0:T(8,128)}, f32[1024,128]{1,0:T(8,128)}, f32[1024,128]{1,0:T(8,128)}, f32[128,1024]{1,0:T(...) custom-call(bf16[256,1024]{1,0:T(8,128)(2,1)} %get-tuple-element.84., ...), custom_call_target="tpu_custom_call" | custom-call | tf_op jit(solution)/shard_map/pallas_call | solution.py:1731
  287.9 0.7 constant_dynamic-slice_fusion
  288.7 0.5 slice_bitcast_fusion
